TPU v7x, 512 devices: a whole 4x8x8 slice. The times are simulated.
512 devices in a mesh: seq: 128 (over z, y, core), head: 4 (over x).
Axes of the slice: x: 4, y: 8, z: 8, core: 2. Of those that a mesh axis runs over, the one named last changes fastest.
Arguments:
- activations: bfloat16 [65536, 1536], P('seq', 'head'), may hold values from -6 to 6
- owners: int32 [256], P('seq'), may hold values from 0 to 127, as said below
- owner_slot: int32 [256], P('seq'), may hold values from 0 to 1, as said below
- counts: int32 [256], P('seq'), may hold values from 1 to 256, as said below
- stale_pairs: bfloat16 [2, 65536, 1536], P(None, 'seq', 'head'), may hold values from -136 to 136
- w_query: bfloat16 [1536, 1536], P(None, 'head'), may hold values from -0.15625 to 0.15625
- w_out: bfloat16 [1536, 1536], P('head'), may hold values from -0.15625 to 0.15625
Outputs:
- mixed: bfloat16 [65536, 1536], P('seq', 'head')
Inputs may be any that keep to these rules, and one draw needn't show every extreme that they name: Window j of device s goes to device owners = (s + o_k) mod 128 with k = owner_slot, for offsets o_k of 1 to 128 - 1 common to all devices, o_0 = 128 - 1; each device receives exactly 2 windows, one in each slot 0 to 1. `owner_slot`: the slots of one device's windows are distinct. `counts`: the first window holds 256 live tokens.
All inputs are finite; a program needn't handle non-finite values.
Results may differ from a plain program's by a relative error of at most 0.03.
Values may be sent and summed in bfloat16 or wider, within the bound.
A program may use at most 64 MiB of HBM per device.

v0:
```python
import jax
import jax.numpy as jnp
from jax import lax
from jax.sharding import PartitionSpec as P

HEAD_DIM = 64


def from_behind(value, axis, by):
    count = lax.axis_size(axis)
    return lax.ppermute(value, axis, [(i, (i + by) % count) for i in range(count)])


def order_windows(source, owners, owner_slot, seq_count):
    window_count = owners.shape[0]
    width = source.shape[0] // window_count * source.shape[1]
    slot_ids = jnp.arange(window_count, dtype=jnp.int32)
    matches = owner_slot[None, :] == slot_ids[:, None]
    placing = matches.astype(jnp.bfloat16)
    ordered = jnp.dot(
        placing, source.reshape(window_count, width), preferred_element_type=jnp.float32
    ).astype(jnp.bfloat16)
    distance = (owners - lax.axis_index("seq")) % seq_count
    slot_offset = jnp.sum(jnp.where(matches, distance[None, :], 0), axis=1)
    return (ordered, slot_offset)


def on_device(activations, owners, owner_slot, counts, stale_pairs, w_query, w_out):
    seq_count = lax.axis_size("seq")
    bit_count = (seq_count - 1).bit_length()
    row_count, col_count = activations.shape
    window_count = owners.shape[0]
    slot_count = row_count // window_count
    heads_here = col_count // HEAD_DIM
    attn_scale = HEAD_DIM ** (-0.5)
    widened = lax.all_gather(activations, "head", axis=1, tiled=True)
    carried, slot_offset = order_windows(widened, owners, owner_slot, seq_count)
    for bit in range(bit_count):
        shifted = from_behind(carried, "seq", 1 << bit)
        taking = slot_offset >> bit & 1 == 1
        carried = jnp.where(taking[:, None], shifted, carried)
    moved_full = carried.reshape(row_count, widened.shape[1])
    moved = lax.dynamic_slice_in_dim(moved_full, lax.axis_index("head") * col_count, col_count, 1)
    query = jnp.dot(moved_full, w_query, preferred_element_type=jnp.float32).astype(jnp.bfloat16)
    query_tiles = query.reshape(window_count, slot_count, heads_here, HEAD_DIM)
    key_tiles = stale_pairs[0].reshape(window_count, slot_count, heads_here, HEAD_DIM)
    value_tiles = stale_pairs[1].reshape(window_count, slot_count, heads_here, HEAD_DIM)
    live_slot = jnp.arange(slot_count, dtype=jnp.int32)[None, :] < counts[:, None]
    live_weight = live_slot.astype(jnp.float32)[:, :, None, None]
    divisor = counts.astype(jnp.float32)[:, None, None]
    pooled_key = (jnp.sum(key_tiles.astype(jnp.float32) * live_weight, axis=1) / divisor).astype(
        jnp.bfloat16
    )
    pooled_value = (
        jnp.sum(value_tiles.astype(jnp.float32) * live_weight, axis=1) / divisor
    ).astype(jnp.bfloat16)
    pooled_key = pooled_key.reshape(window_count, col_count)
    pooled_value = pooled_value.reshape(window_count, col_count)
    fine_scores = (
        jnp.einsum("wqhd,wkhd->whqk", query_tiles, key_tiles, preferred_element_type=jnp.float32)
        * attn_scale
    )
    fine_scores = jnp.where(live_slot[:, None, None, :], fine_scores, -jnp.inf)
    fine_probs = jax.nn.softmax(fine_scores, axis=-1).astype(jnp.bfloat16)
    fine_out = jnp.einsum(
        "whqk,wkhd->wqhd", fine_probs, value_tiles, preferred_element_type=jnp.float32
    )
    fine_out = fine_out.reshape(row_count, heads_here, HEAD_DIM)
    query_heads = jnp.transpose(query.reshape(row_count, heads_here, HEAD_DIM), (1, 0, 2))
    start_state = (
        jnp.full((heads_here, row_count), -jnp.inf, jnp.float32),
        jnp.zeros((heads_here, row_count), jnp.float32),
        jnp.zeros((heads_here, row_count, HEAD_DIM), jnp.float32),
    )
    gathered = (
        lax.all_gather(pooled_key, "seq", axis=0, tiled=True),
        lax.all_gather(pooled_value, "seq", axis=0, tiled=True),
    )
    key_piece = jnp.transpose(gathered[0].reshape(-1, heads_here, HEAD_DIM), (1, 0, 2))
    value_piece = jnp.transpose(gathered[1].reshape(-1, heads_here, HEAD_DIM), (1, 0, 2)).astype(
        jnp.float32
    )

    def per_head(operands):
        head_query, head_key, head_value, old_top, old_mass, old_sum = operands
        head_scores = (
            jnp.dot(head_query, head_key.T, preferred_element_type=jnp.float32) * attn_scale
        )
        new_top = jnp.maximum(old_top, jnp.max(head_scores, axis=1))
        expo_weight = jnp.exp(head_scores - new_top[:, None])
        fading = jnp.exp(old_top - new_top)
        new_mass = old_mass * fading + jnp.sum(expo_weight, axis=1)
        new_sum = old_sum * fading[:, None] + jnp.dot(
            expo_weight, head_value, precision=lax.Precision.HIGHEST
        )
        return (new_top, new_mass, new_sum)

    top_score, weight_mass, value_sum = lax.map(
        per_head,
        (query_heads, key_piece, value_piece, start_state[0], start_state[1], start_state[2]),
    )
    coarse_out = jnp.transpose(value_sum / weight_mass[:, :, None], (1, 0, 2))
    attended = (fine_out + coarse_out).astype(jnp.bfloat16).reshape(row_count, col_count)
    partial_value = jnp.dot(attended, w_out, preferred_element_type=jnp.float32)
    projected = lax.psum_scatter(
        partial_value.astype(jnp.bfloat16), "head", scatter_dimension=1, tiled=True
    ).astype(jnp.float32)
    return (moved.astype(jnp.float32) + projected).astype(jnp.bfloat16)


def solution(mesh):
    placed = (
        P("seq", "head"),
        P("seq"),
        P("seq"),
        P("seq"),
        P(None, "seq", "head"),
        P(None, "head"),
        P("head", None),
    )
    return jax.shard_map(
        on_device, mesh=mesh, in_specs=placed, out_specs=P("seq", "head"), check_vma=False
    )
```

profile of v0, /device:TPU:1, one launch (start us, length us, event | category | flops | bytes accessed | tf_op | source)
XLA Modules:
  0.0 698.7 jit_solution(1849139821743659428)
XLA Ops:
  7.3 39.5 %all-gather.4.cloned.1.call-done = bf16[512,1536]{1,0:T(8,128)(2,1)} async-done(((bf16[512,384]{1,0:T(8,128)(2,1)}), bf16[512,1536]{1,0:T(8,128)(2,1)}) %all-gather.4.cloned.1.call-update) | async-done | bytes 1572880 | tf_op jit(solution)/shard_map/all_gather | solution.py:36
  46.9 3.7 reshape.145
  50.5 3.2 convolution_convert_fusion
  53.7 3.7 collective-permute-start
  58.1 16.7 %collective-permute-done = bf16[2,393216]{1,0:T(2,128)(2,1)} collective-permute-done((bf16[2,393216]{1,0:T(2,128)(2,1)S(1)}, bf16[2,393216]{1,0:T(2,128)(2,1)}, u32[]{:S(2)}, u32[]{:S(2)}) %collective-permute-start) | collective-permute-done | bytes 1572896 | tf_op jit(solution)/shard_map/ppermute | solution.py:11
  74.8 3.4 broadcast_select_fusion
  78.1 3.1 collective-permute-start.1
  81.2 32.6 %collective-permute-done.1 = bf16[2,393216]{1,0:T(2,128)(2,1)S(1)} collective-permute-done((bf16[2,393216]{1,0:T(2,128)(2,1)S(1)}, bf16[2,393216]{1,0:T(2,128)(2,1)S(1)}, u32[]{:S(2)}, u32[]{:S(2)}) %collective-permute-start.1) | collective-permute-done | bytes 1572896 | tf_op jit(solution)/shard_map/ppermute | solution.py:11
  113.8 1.9 broadcast_select_fusion.1
  115.7 6.2 collective-permute-start.2
  121.9 33.6 %collective-permute-done.2 = bf16[2,393216]{1,0:T(2,128)(2,1)S(1)} collective-permute-done((bf16[2,393216]{1,0:T(2,128)(2,1)S(1)}, bf16[2,393216]{1,0:T(2,128)(2,1)S(1)}, u32[]{:S(2)}, u32[]{:S(2)}) %collective-permute-start.2) | collective-permute-done | bytes 1572896 | tf_op jit(solution)/shard_map/ppermute | solution.py:11
  155.5 1.9 broadcast_select_fusion.2
  157.4 2.0 collective-permute-start.3
  159.4 104.0 %collective-permute-done.3 = bf16[2,393216]{1,0:T(2,128)(2,1)S(1)} collective-permute-done((bf16[2,393216]{1,0:T(2,128)(2,1)S(1)}, bf16[2,393216]{1,0:T(2,128)(2,1)S(1)}, u32[]{:S(2)}, u32[]{:S(2)}) %collective-permute-start.3) | collective-permute-done | bytes 1572896 | tf_op jit(solution)/shard_map/ppermute | solution.py:11
  263.4 1.9 broadcast_select_fusion.3
  265.3 1.9 collective-permute-start.4
  267.3 35.7 %collective-permute-done.4 = bf16[2,393216]{1,0:T(2,128)(2,1)S(1)} collective-permute-done((bf16[2,393216]{1,0:T(2,128)(2,1)S(1)}, bf16[2,393216]{1,0:T(2,128)(2,1)S(1)}, u32[]{:S(2)}, u32[]{:S(2)}) %collective-permute-start.4) | collective-permute-done | bytes 1572896 | tf_op jit(solution)/shard_map/ppermute | solution.py:11
  303.0 1.9 broadcast_select_fusion.4
  304.9 1.9 collective-permute-start.5
  306.8 69.4 %collective-permute-done.5 = bf16[2,393216]{1,0:T(2,128)(2,1)S(1)} collective-permute-done((bf16[2,393216]{1,0:T(2,128)(2,1)S(1)}, bf16[2,393216]{1,0:T(2,128)(2,1)S(1)}, u32[]{:S(2)}, u32[]{:S(2)}) %collective-permute-start.5) | collective-permute-done | bytes 1572896 | tf_op jit(solution)/shard_map/ppermute | solution.py:11
  376.3 1.9 broadcast_select_fusion.5
  378.2 3.6 collective-permute-start.6
  381.8 1.9 fusion.30
  386.1 1.2 convert_element_type.72
  387.3 1.3 fusion.28
  388.6 1.9 multiply_reduce_fusion
  392.1 175.9 %all-gather = bf16[128,2,384]{2,1,0:T(2,128)(2,1)S(1)} all-gather(bf16[1,2,384]{2,1,0:T(2,128)(2,1)S(1)} %get-tuple-element.79), channel_id=1, replica_groups=mesh['seq'=128,'head'=4] {'seq'}, dimensions={0}, use_global_device_ids=true | all-gather | bytes 198144 | tf_op jit(solution)/shard_map/all_gather | solution.py:76
  569.1 1.8 copy.43
  571.0 50.5 %all-gather.1 = bf16[128,2,384]{2,1,0:T(2,128)(2,1)S(1)} all-gather(bf16[1,2,384]{2,1,0:T(2,128)(2,1)S(1)} %get-tuple-element.78), channel_id=1, replica_groups=mesh['seq'=128,'head'=4] {'seq'}, dimensions={0}, use_global_device_ids=true | all-gather | bytes 198144 | tf_op jit(solution)/shard_map/all_gather | solution.py:77
  621.4 1.2 reshape.152
  622.7 4.3 broadcast_select_fusion.6
  627.0 2.9 reshape.146
  629.9 2.7 convolution_convert_fusion.2
  633.4 1.6 fusion.19
  637.1 22.8 %while.12 = (s32[]{:T(128)}, f32[6,512]{1,0:T(8,128)S(1)}, f32[6,512,64]{1,2,0:T(8,128)}, bf16[6,512,64]{2,1,0:T(8,128)(2,1)S(1)}, bf16[6,256,64]{2,1,0:T(8,128)...) while((s32[]{:T(128)}, f32[6,512]{1,0:T(8,128)S(1)}, f32[6,512,64]{1,2,0:T(8,128)}, ...), condition=%wide.region_8.9_spmd, body=%wide.region_5.8_spmd.sunk | while | flops 118129152 | bytes 2120809 | solution.py:98
  638.4 1.3 constant_dynamic-slice_fusion.2
  642.2 1.3 constant_dynamic-slice_fusion.2
  646.0 1.3 constant_dynamic-slice_fusion.2
  649.8 1.3 constant_dynamic-slice_fusion.2
  651.1 1.2 fusion.45
  653.6 1.3 constant_dynamic-slice_fusion.2
  657.4 1.3 constant_dynamic-slice_fusion.2
  658.7 1.2 fusion.45
  659.9 1.3 fusion.17
  662.3 1.6 copy.48
  663.9 24.9 %reduce-scatter.4.cloned.1.call-done = bf16[384,512]{1,0:T(8,128)(2,1)} async-done(((bf16[1536,512]{1,0:T(8,128)(2,1)}), bf16[384,512]{1,0:T(8,128)(2,1)}) %reduce-scatter.4.cloned.1.call-update) | async-done | bytes 393232
  688.8 1.2 copy.49
  690.0 1.8 add_convert_fusion
  (66 shorter events, 22.5 us)
Async XLA Ops:
  6.5 654.7 %copy-start = (bf16[384,1536]{1,0:T(8,128)(2,1)S(1)}, bf16[384,1536]{1,0:T(8,128)(2,1)}, u32[]{:S(2)}) copy-start(bf16[384,1536]{1,0:T(8,128)(2,1)} %param.15) | copy-start | bytes 3538948
  6.5 40.3 %all-gather.4.cloned.1.call-start = ((), (), s32[]{:S(2)}) async-start(), calls=%async_computation.1 | async-start | bytes 1966080 | tf_op jit(solution)/shard_map/all_gather | solution.py:36
  7.3 43.3 %copy-start.6 = (s32[2]{0:T(128)S(1)}, s32[2]{0:T(128)}, u32[]{:S(2)}) copy-start(s32[2]{0:T(128)} %param.11) | copy-start | bytes 28
  7.3 681.5 %reduce-scatter.4.cloned.1.call-start = ((), (), s32[]{:S(2)}) async-start(), calls=%async_computation.2 | async-start | bytes 1966080
  50.5 6.9 copy-start.5
  53.7 21.0 %collective-permute-start = (bf16[2,393216]{1,0:T(2,128)(2,1)S(1)}, bf16[2,393216]{1,0:T(2,128)(2,1)}, u32[]{:S(2)}, u32[]{:S(2)}) collective-permute-start(bf16[2,393216]{1,0:T(2,128)(2,1)S(1)} %convolution_convert_fusion), channel_id=1, source_target_pairs={{0,4},{4,8},{8,12},{12,16},{16,20},{20,24},{24,28},{28,32},{32,36}... | collective-permute-start | bytes 4718600 | tf_op jit(solution)/shard_map/ppermute | solution.py:11
  78.1 35.7 %collective-permute-start.1 = (bf16[2,393216]{1,0:T(2,128)(2,1)S(1)}, bf16[2,393216]{1,0:T(2,128)(2,1)S(1)}, u32[]{:S(2)}, u32[]{:S(2)}) collective-permute-start(bf16[2,393216]{1,0:T(2,128)(2,1)S(1)} %broadcast_select_fusion), channel_id=1, source_target_pairs={{0,8},{4,12},{8,16},{12,20},{16,24},{20,28},{24,32},{28,36},{32,40... | collective-permute-start | bytes 4718600 | tf_op jit(solution)/shard_map/ppermute | solution.py:11
  115.7 39.8 %collective-permute-start.2 = (bf16[2,393216]{1,0:T(2,128)(2,1)S(1)}, bf16[2,393216]{1,0:T(2,128)(2,1)S(1)}, u32[]{:S(2)}, u32[]{:S(2)}) collective-permute-start(bf16[2,393216]{1,0:T(2,128)(2,1)S(1)} %broadcast_select_fusion.1), channel_id=1, source_target_pairs={{0,16},{4,20},{8,24},{12,28},{16,32},{20,36},{24,40},{28,44},{32,4... | collective-permute-start | bytes 4718600 | tf_op jit(solution)/shard_map/ppermute | solution.py:11
  157.4 106.0 %collective-permute-start.3 = (bf16[2,393216]{1,0:T(2,128)(2,1)S(1)}, bf16[2,393216]{1,0:T(2,128)(2,1)S(1)}, u32[]{:S(2)}, u32[]{:S(2)}) collective-permute-start(bf16[2,393216]{1,0:T(2,128)(2,1)S(1)} %broadcast_select_fusion.2), channel_id=1, source_target_pairs={{0,32},{4,36},{8,40},{12,44},{16,48},{20,52},{24,56},{28,60},{32,6... | collective-permute-start | bytes 4718600 | tf_op jit(solution)/shard_map/ppermute | solution.py:11
  265.3 37.6 %collective-permute-start.4 = (bf16[2,393216]{1,0:T(2,128)(2,1)S(1)}, bf16[2,393216]{1,0:T(2,128)(2,1)S(1)}, u32[]{:S(2)}, u32[]{:S(2)}) collective-permute-start(bf16[2,393216]{1,0:T(2,128)(2,1)S(1)} %broadcast_select_fusion.3), channel_id=1, source_target_pairs={{0,64},{4,68},{8,72},{12,76},{16,80},{20,84},{24,88},{28,92},{32,9... | collective-permute-start | bytes 4718600 | tf_op jit(solution)/shard_map/ppermute | solution.py:11
  304.9 71.4 %collective-permute-start.5 = (bf16[2,393216]{1,0:T(2,128)(2,1)S(1)}, bf16[2,393216]{1,0:T(2,128)(2,1)S(1)}, u32[]{:S(2)}, u32[]{:S(2)}) collective-permute-start(bf16[2,393216]{1,0:T(2,128)(2,1)S(1)} %broadcast_select_fusion.4), channel_id=1, source_target_pairs={{0,128},{4,132},{8,136},{12,140},{16,144},{20,148},{24,152},{28,15... | collective-permute-start | bytes 4718600 | tf_op jit(solution)/shard_map/ppermute | solution.py:11
  378.2 244.5 %collective-permute-start.6 = (bf16[2,393216]{1,0:T(2,128)(2,1)S(1)}, bf16[2,393216]{1,0:T(2,128)(2,1)}, u32[]{:S(2)}, u32[]{:S(2)}) collective-permute-start(bf16[2,393216]{1,0:T(2,128)(2,1)S(1)} %broadcast_select_fusion.5), channel_id=1, source_target_pairs={{0,256},{4,260},{8,264},{12,268},{16,272},{20,276},{24,280},{28,28... | collective-permute-start | bytes 4718600 | tf_op jit(solution)/shard_map/ppermute | solution.py:11
  568.0 54.7 %copy-start.3 = (pred[2]{0:T(512)(128)(4,1)S(1)}, pred[2]{0:T(512)(128)(4,1)}, u32[]{:S(2)}) copy-start(pred[2]{0:T(512)(128)(4,1)} %get-tuple-element.82) | copy-start | bytes 10
  629.9 2.7 copy-start.1
  633.4 1.6 copy-start.4
  635.1 1.2 copy-start.2
Sparse Core Ops, SparseCore 0:
  9.5 37.3 all-gather.3
  664.0 24.7 reduce-scatter.3
where the time goes:
time: 700 us; the launch traced here: 699 us
  waiting for transfers between devices  357 us (51%)
  blocking collectives  226 us (32%)
  local copies, waits for them, and re-layouts  28.3 us (4%)
  other arithmetic  28.2 us (4%)
  starting transfers between devices  22.4 us (3%)
  matrix products  22.4 us (3%)
  between operations  13.7 us (2%)
    ppermute x7, waiting for transfers between devices, from_behind(): lax.ppermute(value, axis, [(i, (i + by) % count) for i in range(count)])  292 us
    all_gather x1, blocking collectives, on_device(): lax.all_gather(pooled_key, 'seq', axis=0, tiled=True)  176 us
    all_gather x1, blocking collectives, on_device(): lax.all_gather(pooled_value, 'seq', axis=0, tiled=True)  50.5 us
    all_gather x1, waiting for transfers between devices, on_device(): widened = lax.all_gather(activations, 'head', axis=1, tiled=True)  39.5 us
    unnamed x3, waiting for transfers between devices  25.6 us
    ppermute x7, starting transfers between devices, from_behind(): lax.ppermute(value, axis, [(i, (i + by) % count) for i in range(count)])  22.4 us
    select_n x7, other arithmetic, on_device(): carried = jnp.where(taking[:, None], shifted, carried)  17.3 us
  transfers between devices with their start and end apart: 9, of which 8 were waited for; matrix products, arithmetic and copies ran while one was open for 2% of the time, Pallas kernels for 0%

commit v1 on v0

v1 whole, which is shorter than its diff:
```python
import functools

import jax
import jax.numpy as jnp
from jax import lax
from jax.experimental import pallas as pl
from jax.experimental.pallas import tpu as pltpu
from jax.sharding import PartitionSpec as P

HEAD_DIM = 64
PAIR = 2 * HEAD_DIM
Y_CHIPS = 8
CHUNK = 128
MESH = pl.DeviceIdType.MESH
F32 = jnp.float32
BF16 = jnp.bfloat16


def attention_kernel(
    seq_count,
    rows,
    counts,
    first,
    second,
    stale_hbm,
    wq_hbm,
    wo_hbm,
    out,
    xg,
    stale,
    wq,
    wo,
    stage,
    pool,
    pool_wide,
    kcat,
    vaug,
    q_s,
    att_s,
    p_opp,
    p_right,
    p_left,
    p_own,
    in_opp_left,
    in_opp_right,
    in_left,
    in_right,
    load_sem,
    x_send,
    x_recv,
    rs_send,
    rs_recv,
    pool_send,
    pool_recv,
):
    width = xg.shape[2]
    total = xg.shape[1]
    chunks = total // CHUNK
    half = CHUNK // 2
    pairs = width // PAIR
    per_window = rows // CHUNK
    z_chips = seq_count // (2 * Y_CHIPS)
    seq = lax.axis_index("seq")
    head = lax.axis_index("head")
    heads = lax.axis_size("head")
    core = lax.rem(seq, 2)
    y = lax.rem(lax.div(seq, 2), Y_CHIPS)
    z = lax.div(seq, 2 * Y_CHIPS)
    right = (seq, lax.rem(head + 1, heads))
    left = (seq, lax.rem(head + heads - 1, heads))
    other_core = (seq + 1 - 2 * core, head)
    inner = y + core * (z - y)
    outer = z + core * (y - z)
    inner_step = 2 + core * (2 * Y_CHIPS - 2)
    outer_step = 2 * Y_CHIPS - core * (2 * Y_CHIPS - 2)
    ring = z_chips

    def inner_peer(j):
        return (seq + (lax.rem(inner + j, ring) - inner) * inner_step, head)

    def outer_peer(j):
        return (seq + (lax.rem(outer + j, ring) - outer) * outer_step, head)

    loads = [
        pltpu.make_async_copy(stale_hbm, stale, load_sem.at[0]),
        pltpu.make_async_copy(wq_hbm, wq, load_sem.at[1]),
        pltpu.make_async_copy(wo_hbm, wo, load_sem.at[2]),
        pltpu.make_async_copy(first, xg.at[0, pl.ds(0, rows)], load_sem.at[3]),
        pltpu.make_async_copy(second, xg.at[0, pl.ds(rows, rows)], load_sem.at[4]),
    ]
    loads[0].start()
    loads[3].start()
    loads[4].start()
    loads[1].start()
    loads[2].start()

    barrier = pltpu.get_barrier_semaphore()
    peers = [left, right, other_core]
    peers += [inner_peer(j) for j in range(1, ring)]
    peers += [outer_peer(j) for j in range(1, ring)]
    for peer in peers:
        pl.semaphore_signal(barrier, inc=1, device_id=peer, device_id_type=MESH)
    pl.semaphore_wait(barrier, len(peers))

    def remote(src, dst, send, recv, peer):
        return pltpu.make_async_remote_copy(
            src_ref=src,
            dst_ref=dst,
            send_sem=send,
            recv_sem=recv,
            device_id=peer,
            device_id_type=MESH,
        )

    def direct(c, src, way):
        peer, slot = ((right, 1), (left, 3))[way]
        return remote(
            src,
            xg.at[slot, pl.ds(c * CHUNK, CHUNK)],
            x_send.at[way, c],
            x_recv.at[way, c],
            peer,
        )

    def forward(c, way):
        peer, slot = ((right, 1), (left, 3))[way]
        part = pl.ds(pl.multiple_of(c * CHUNK + way * half, half), half)
        return remote(
            xg.at[slot, part],
            xg.at[2, part],
            x_send.at[2 + way, c],
            x_recv.at[2 + way, c],
            peer,
        )

    sent = []
    for c in range(chunks):
        ref, at = (first, c) if c < per_window else (second, c - per_window)
        for way in range(2):
            copy = direct(c, ref.at[pl.ds(at * CHUNK, CHUNK)], way)
            copy.start()
            sent.append(copy)

    loads[0].wait()
    stage[...] = jnp.zeros_like(stage)
    row_ids = lax.broadcasted_iota(jnp.int32, (rows, width), 0)
    for kind in range(2):
        for w in range(2):
            count = counts[w]
            part = stale[kind, pl.ds(w * rows, rows), :].astype(F32)
            part = jnp.where(row_ids < count, part, 0.0)
            mean = jnp.sum(part, axis=0, keepdims=True) / count.astype(F32)
            for t in range(pairs):
                at = (kind * 2 + w) * pairs + t
                stage[pl.ds(at, 1), :] = mean[:, t * PAIR : (t + 1) * PAIR]
    pool[core, outer, inner] = stage[...].astype(BF16)

    def inner_copy(j, which):
        ref = pool.at[core, outer, which]
        return remote(ref, ref, pool_send.at[j - 1], pool_recv.at[j - 1], inner_peer(j))

    def outer_copy(j, which):
        ref = pool.at[core, which]
        at = ring + j - 2
        return remote(ref, ref, pool_send.at[at], pool_recv.at[at], outer_peer(j))

    def core_copy(which):
        ref = pool.at[which]
        at = 2 * ring - 2
        return remote(ref, ref, pool_send.at[at], pool_recv.at[at], other_core)

    for j in range(1, ring):
        inner_copy(j, inner).start()

    lanes = lax.broadcasted_iota(jnp.int32, (1, PAIR), 1)
    keep = [
        jnp.where(lanes < HEAD_DIM, 1.0, 0.0),
        jnp.where(lanes < HEAD_DIM, 0.0, 1.0),
    ]

    def lay_out(at, p, key, value):
        for which in range(2):
            part = pl.ds(which * rows, rows)
            kcat[at, p, part, :] = (key * keep[which]).astype(BF16)
            vaug[at, p, part, 0:PAIR] = (value * keep[which]).astype(BF16)
            vaug[at, p, part, PAIR : 2 * PAIR] = jnp.broadcast_to(
                keep[which], (rows, PAIR)
            ).astype(BF16)

    for w in range(2):
        for p in range(pairs):
            cols = slice(p * PAIR, (p + 1) * PAIR)
            lay_out(
                w,
                p,
                stale[0, pl.ds(w * rows, rows), cols].astype(F32),
                stale[1, pl.ds(w * rows, rows), cols].astype(F32),
            )

    def pass_on(c):
        for way in range(2):
            direct(c, xg.at[0, pl.ds(c * CHUNK, CHUNK)], way).wait_recv()
            forward(c, way).start()

    pass_on(0)

    for j in range(1, ring):
        inner_copy(j, lax.rem(inner + ring - j, ring)).wait_recv()
    for j in range(1, ring):
        outer_copy(j, outer).start()

    loads[1].wait()
    loads[2].wait()
    loads[3].wait()
    loads[4].wait()

    for j in range(1, ring):
        outer_copy(j, lax.rem(outer + ring - j, ring)).wait_recv()
    core_copy(core).start()
    pass_on(1)
    core_copy(1 - core).wait_recv()

    for i in range(2):
        for j in range(ring):
            at = (i * ring + j) * ring * 16
            pool_wide[pl.ds(at, ring * 16), :] = (
                pool[i, j].reshape(ring * 16, PAIR).astype(F32)
            )
    for p in range(pairs):
        pooled = []
        for kind in range(2):
            pieces = [
                pool_wide[pl.ds((kind * 2 + w) * pairs + p, seq_count, stride=16), :]
                for w in range(2)
            ]
            pooled.append(jnp.concatenate(pieces, axis=0))
        lay_out(2, p, pooled[0], pooled[1])

    def opp_copy(c, way):
        peer = (right, left)[way]
        dst = (in_opp_left, in_opp_right)[way]
        part = pl.ds(way * half, half)
        return remote(
            p_opp.at[c, part], dst.at[c], rs_send.at[way, c], rs_recv.at[way, c], peer
        )

    def share_copy(c, way, piece):
        peer = (right, left)[way]
        src = (p_right, p_left)[way]
        dst = (in_left, in_right)[way]
        part = pl.ds(piece * half, half)
        at = 2 + 2 * way + piece
        return remote(
            src.at[c, part], dst.at[c, part], rs_send.at[at, c], rs_recv.at[at, c], peer
        )

    def relay(c):
        for way in range(2):
            opp_copy(c, way).wait_recv()
            src = (p_right, p_left)[way]
            add = (in_opp_left, in_opp_right)[way]
            part = pl.ds(way * half, half)
            src[c, part, :] = (src[c, part, :].astype(F32) + add[c].astype(F32)).astype(BF16)
            share_copy(c, way, way).start()

    def softmax_out(at, p, query, bias):
        scores = lax.dot_general(
            query, kcat[at, p], (((1,), (1,)), ((), ())), preferred_element_type=F32
        )
        parts = []
        for which in range(2):
            part = scores[:, which * rows : (which + 1) * rows]
            if bias is not None:
                part = part + bias
            top = jnp.max(part, axis=1, keepdims=True)
            parts.append(jnp.exp(part - top).astype(BF16))
        both = jnp.dot(
            jnp.concatenate(parts, axis=1), vaug[at, p], preferred_element_type=F32
        )
        return both[:, 0:PAIR] / both[:, PAIR : 2 * PAIR]

    def step(c, carry):
        @pl.when(jnp.logical_and(c >= 1, c + 1 < chunks))
        def _():
            pass_on(c + 1)

        for way in range(2):
            forward(c, way).wait_recv()
        here = pl.ds(pl.multiple_of(c * CHUNK, CHUNK), CHUNK)
        query = None
        for r in range(4):
            source = lax.rem(head + heads - r, heads)
            w_rows = pl.ds(pl.multiple_of(source * width, width), width)
            term = jnp.dot(xg[r, here, :], wq[w_rows, :], preferred_element_type=F32)
            query = term if query is None else query + term
        q_s[...] = (query.astype(BF16).astype(F32) * HEAD_DIM ** (-0.5)).astype(BF16)
        w = lax.div(c, per_window)
        slots = lax.broadcasted_iota(jnp.int32, (1, rows), 1)
        bias = jnp.where(slots < counts[w], 0.0, -1e30)

        def pair(p, inner_carry):
            cols = pl.ds(pl.multiple_of(p * PAIR, PAIR), PAIR)
            q_p = q_s[:, cols]
            fine = softmax_out(w, p, q_p, bias)
            coarse = softmax_out(2, p, q_p, None)
            att_s[:, cols] = (fine + coarse).astype(BF16)
            return inner_carry

        lax.fori_loop(0, pairs, pair, 0)

        def project(r):
            target = lax.rem(head + r, heads)
            cols = pl.ds(pl.multiple_of(target * width, PAIR), width)
            return jnp.dot(att_s[...], wo[:, cols], preferred_element_type=F32).astype(BF16)

        p_opp[c] = project(2)
        opp_copy(c, 0).start()
        opp_copy(c, 1).start()
        p_right[c] = project(1)
        share_copy(c, 0, 1).start()
        p_left[c] = project(3)
        share_copy(c, 1, 0).start()
        p_own[c] = project(0)

        @pl.when(c >= 1)
        def _():
            relay(c - 1)

        return carry

    lax.fori_loop(0, chunks, step, 0)
    relay(chunks - 1)

    def finish(c, carry):
        for way in range(2):
            for piece in range(2):
                share_copy(c, way, piece).wait_recv()
        here = pl.ds(pl.multiple_of(c * CHUNK, CHUNK), CHUNK)
        projected = (
            p_own[c].astype(F32) + in_left[c].astype(F32) + in_right[c].astype(F32)
        )
        out[here, :] = (xg[0, here, :].astype(F32) + projected).astype(BF16)
        return carry

    lax.fori_loop(0, chunks, finish, 0)

    for copy in sent:
        copy.wait_send()
    for c in range(chunks):
        for way in range(2):
            forward(c, way).wait_send()
            opp_copy(c, way).wait_send()
            for piece in range(2):
                share_copy(c, way, piece).wait_send()
    for j in range(1, ring):
        inner_copy(j, inner).wait_send()
        outer_copy(j, outer).wait_send()
    core_copy(core).wait_send()


def on_device(activations, owners, owner_slot, counts, stale_pairs, w_query, w_out):
    seq_count = lax.axis_size("seq")
    total, width = activations.shape
    rows = total // owners.shape[0]
    chunks = total // CHUNK
    half = CHUNK // 2
    pairs = width // PAIR
    ring = Y_CHIPS
    in_order = owner_slot[0] == 0
    slot_0 = jnp.where(in_order, activations[:rows], activations[rows:])
    slot_1 = jnp.where(in_order, activations[rows:], activations[:rows])
    owner_1 = jnp.where(in_order, owners[1], owners[0])
    offset = (owner_1 - lax.axis_index("seq")) % seq_count

    def shift(value, by):
        return lax.ppermute(
            value, "seq", [(i, (i + by) % seq_count) for i in range(seq_count)]
        )

    first = shift(slot_0, seq_count - 1)
    second = lax.switch(
        offset - 1,
        [functools.partial(shift, by=by) for by in range(1, seq_count)],
        slot_1,
    )
    hbm = pl.BlockSpec(memory_space=pl.ANY)
    dma = pltpu.SemaphoreType.DMA
    return pl.pallas_call(
        functools.partial(attention_kernel, seq_count, rows),
        out_shape=jax.ShapeDtypeStruct((total, width), BF16),
        in_specs=[pl.BlockSpec(memory_space=pltpu.SMEM)] + [hbm] * 5,
        out_specs=pl.BlockSpec(memory_space=pltpu.VMEM),
        scratch_shapes=[
            pltpu.VMEM((4, total, width), BF16),
            pltpu.VMEM(stale_pairs.shape, BF16),
            pltpu.VMEM(w_query.shape, BF16),
            pltpu.VMEM(w_out.shape, BF16),
            pltpu.VMEM((16, PAIR), F32),
            pltpu.VMEM((2, ring, ring, 16, PAIR), BF16),
            pltpu.VMEM((2 * ring * ring * 16, PAIR), F32),
            pltpu.VMEM((3, pairs, 2 * rows, PAIR), BF16),
            pltpu.VMEM((3, pairs, 2 * rows, 2 * PAIR), BF16),
            pltpu.VMEM((CHUNK, width), BF16),
            pltpu.VMEM((CHUNK, width), BF16),
            pltpu.VMEM((chunks, CHUNK, width), BF16),
            pltpu.VMEM((chunks, CHUNK, width), BF16),
            pltpu.VMEM((chunks, CHUNK, width), BF16),
            pltpu.VMEM((chunks, CHUNK, width), BF16),
            pltpu.VMEM((chunks, half, width), BF16),
            pltpu.VMEM((chunks, half, width), BF16),
            pltpu.VMEM((chunks, CHUNK, width), BF16),
            pltpu.VMEM((chunks, CHUNK, width), BF16),
            dma((5,)),
            dma((4, chunks)),
            dma((4, chunks)),
            dma((6, chunks)),
            dma((6, chunks)),
            dma((2 * ring - 1,)),
            dma((2 * ring - 1,)),
        ],
        compiler_params=pltpu.CompilerParams(
            collective_id=0, has_side_effects=True, vmem_limit_bytes=40 * 1024 * 1024
        ),
        name="window_attention",
    )(counts, first, second, stale_pairs, w_query, w_out)


def solution(mesh):
    placed = (
        P("seq", "head"),
        P("seq"),
        P("seq"),
        P("seq"),
        P(None, "seq", "head"),
        P(None, "head"),
        P("head", None),
    )
    return jax.shard_map(
        on_device, mesh=mesh, in_specs=placed, out_specs=P("seq", "head"), check_vma=False
    )
```

time: 700 us -> 123 us (0.18)
  waiting for transfers between devices: 357 us -> 21.9 us
  blocking collectives: 226 us -> 0 us
  Pallas kernels: 0 us -> 55.9 us
  other arithmetic: 28.2 us -> 1.06 us
  local copies, waits for them, and re-layouts: 28.3 us -> 5.33 us
  matrix products: 22.4 us -> 0 us
  starting transfers between devices: 22.4 us -> 36.3 us
  between operations: 13.7 us -> 2.14 us
    ppermute x7 -> x2, waiting for transfers between devices: 292 us -> 21.9 us  [shift(): lax.ppermute(value, 'seq', [(i, (i + by) % seq_count) for i in range(seq_...]
    all_gather x2 -> x0, blocking collectives: 226 us -> none  [the longest x1 176 us: on_device(): lax.all_gather(pooled_key, 'seq', axis=0, tiled=True)]
    pallas_call x0 -> x1, Pallas kernels: none -> 55.9 us  [on_device(): pl.pallas_call(functools.partial(attention_kernel, seq_count, rows), out_...]
    all_gather x1 -> x0, waiting for transfers between devices: 39.5 us -> none  [on_device(): widened = lax.all_gather(activations, 'head', axis=1, tiled=True)]
    unnamed x3 -> x0, waiting for transfers between devices: 25.6 us -> none
    dot_general x17 -> x0, matrix products: 22.4 us -> none  [the longest x6 7.02 us: per_head(): jnp.dot(expo_weight, head_value, precision=lax.Precision.HIGHEST)]
    select_n x8 -> x1, other arithmetic: 17.3 us -> 1.06 us  [on_device(): slot_1 = jnp.where(in_order, activations[rows:], activations[:rows])]
    ppermute x7 -> x2, starting transfers between devices: 22.4 us -> 36.3 us  [shift(): lax.ppermute(value, 'seq', [(i, (i + by) % seq_count) for i in range(seq_...]
  transfers between devices with their start and end apart: 9 -> 2, of which waited for: 8 -> 1; matrix products, arithmetic and copies ran while one was open for 2% -> 1% of each run, Pallas kernels for 0% -> 0%
where the time goes in v1:
time: 123 us
  Pallas kernels  55.9 us (45%)
  starting transfers between devices  36.3 us (30%)
  waiting for transfers between devices  21.9 us (18%)
  local copies, waits for them, and re-layouts  5.33 us (4%)
  between operations  2.14 us (2%)
    pallas_call x1, Pallas kernels, on_device(): pl.pallas_call(functools.partial(attention_kernel, seq_count, rows), out_...  55.9 us
    ppermute x2, starting transfers between devices, shift(): lax.ppermute(value, 'seq', [(i, (i + by) % seq_count) for i in range(seq_...  36.3 us
    ppermute x2, waiting for transfers between devices, shift(): lax.ppermute(value, 'seq', [(i, (i + by) % seq_count) for i in range(seq_...  21.9 us
    unnamed x9, local copies, waits for them, and re-layouts  3.95 us
  transfers between devices with their start and end apart: 2, of which 1 were waited for; matrix products, arithmetic and copies ran while one was open for 1% of the time, Pallas kernels for 0%

profile of v1, /device:TPU:1, one launch (start us, length us, event | category | flops | bytes accessed | tf_op | source)
XLA Modules:
  0.0 122.7 jit_solution(12052676736316512189)
XLA Ops:
  0.0 0.0 copy-start.2
  0.7 1.1 broadcast_select_fusion
  1.8 19.5 %collective-permute-start.127 = (bf16[256,384]{1,0:T(8,128)(2,1)S(1)}, bf16[256,384]{1,0:T(8,128)(2,1)S(1)}, u32[]{:S(2)}, u32[]{:S(2)}) collective-permute-start(bf16[256,384]{1,0:T(8,128)(2,1)S(1)} %get-tuple-element.261), channel_id=1, source_target_pairs={{0,508},{4,0},{8,4},{12,8},{16,12},{20,16},{24,20},{28,24},{32,28}... | collective-permute-start | bytes 589832 | tf_op jit(solution)/shard_map/ppermute | solution.py:376
  21.4 1.4 %fusion = (s32[1]{0:T(128)}, s32[1]{0:T(128)}) fusion(s32[2]{0:T(128)} %param.135), kind=kLoop, calls=%fused_computation.2 | loop fusion | bytes 16 | tf_op jit(solution)/shard_map/slice | solution.py:372
  24.1 38.7 %conditional.1 = (bf16[256,384]{1,0:T(8,128)(2,1)}) conditional(s32[]{:T(128)} %clamp.3, bf16[256,384]{1,0:T(8,128)(2,1)S(1)} %get-tuple-element.260, bf16[256,384]{1,0:T(8,128)(2,1)S(1)} %get-tuple-element.260, bf16[256,384]{1,0:T(8,128)(2,1)S(1)} %get-tuple-element.260, ...), branch_computations={%region_0.1_spmd, %region_1.2_spmd, %region_2.3_spmd, %region_3.4_... | conditional | bytes 786480 | solution.py:381
  24.2 16.7 %collective-permute-start.68 = (bf16[256,384]{1,0:T(8,128)(2,1)S(1)}, bf16[256,384]{1,0:T(8,128)(2,1)}, u32[]{:S(2)}, u32[]{:S(2)}) collective-permute-start(bf16[256,384]{1,0:T(8,128)(2,1)S(1)} %param.68), channel_id=1, source_target_pairs={{0,276},{4,280},{8,284},{12,288},{16,292},{20,296},{24,300},{28,30... | collective-permute-start | bytes 589832 | tf_op jit(solution)/shard_map/cond/branch_68_fun/ppermute | solution.py:376
  40.9 21.9 %collective-permute-done.68 = bf16[256,384]{1,0:T(8,128)(2,1)} collective-permute-done((bf16[256,384]{1,0:T(8,128)(2,1)S(1)}, bf16[256,384]{1,0:T(8,128)(2,1)}, u32[]{:S(2)}, u32[]{:S(2)}) %collective-permute-start.68) | collective-permute-done | bytes 196640 | tf_op jit(solution)/shard_map/cond/branch_68_fun/ppermute | solution.py:376
  62.8 0.0 collective-permute-done.127.first
  62.8 0.0 copy-done.2
  62.8 0.0 copy-start
  62.8 1.3 %copy-done = bf16[1536,384]{1,0:T(8,128)(2,1)S(1)} copy-done((bf16[1536,384]{1,0:T(8,128)(2,1)S(1)}, bf16[1536,384]{1,0:T(8,128)(2,1)}, u32[]{:S(2)}) %copy-start) | copy-done | bytes 1179672
  64.1 0.0 copy-start.1
  64.1 1.3 %copy-done.1 = bf16[384,1536]{1,0:T(8,128)(2,1)S(1)} copy-done((bf16[384,1536]{1,0:T(8,128)(2,1)S(1)}, bf16[384,1536]{1,0:T(8,128)(2,1)}, u32[]{:S(2)}) %copy-start.1) | copy-done | bytes 1179672
  65.4 0.0 copy-start.3
  65.4 0.7 copy-done.3
  66.0 55.9 %window_attention.1 = bf16[512,384]{1,0:T(8,128)(2,1)S(1)} custom-call(s32[2]{0:T(128)S(1)} %copy-done.3, bf16[256,384]{1,0:T(8,128)(2,1)S(1)} %collective-permute-done.127.first, bf16[256,384]{1,0:T(8,128)(2,1)} %get-tuple-element.264.second, bf16[2,512,384]{2,1,0:T(8,128)(2,1)S(1)} %copy-done.2, bf16[1536,384]{1,0:T(8,128)(2,1)S(1)} %copy-done, ...), custom_call_target="tpu_custom_call" | custom-call | tf_op jit(solution)/shard_map/window_attention/pallas_call | solution.py:388
  121.9 0.7 copy.136
Async XLA Ops:
  0.0 62.8 %copy-start.2 = (bf16[2,512,384]{2,1,0:T(8,128)(2,1)S(1)}, bf16[2,512,384]{2,1,0:T(8,128)(2,1)}, u32[]{:S(2)}) copy-start(bf16[2,512,384]{2,1,0:T(8,128)(2,1)} %stale_hbm.1) | copy-start | bytes 2359300
  1.8 61.0 %collective-permute-start.127 = (bf16[256,384]{1,0:T(8,128)(2,1)S(1)}, bf16[256,384]{1,0:T(8,128)(2,1)S(1)}, u32[]{:S(2)}, u32[]{:S(2)}) collective-permute-start(bf16[256,384]{1,0:T(8,128)(2,1)S(1)} %get-tuple-element.261), channel_id=1, source_target_pairs={{0,508},{4,0},{8,4},{12,8},{16,12},{20,16},{24,20},{28,24},{32,28}... | collective-permute-start | bytes 589832 | tf_op jit(solution)/shard_map/ppermute | solution.py:376
  24.2 38.7 %collective-permute-start.68 = (bf16[256,384]{1,0:T(8,128)(2,1)S(1)}, bf16[256,384]{1,0:T(8,128)(2,1)}, u32[]{:S(2)}, u32[]{:S(2)}) collective-permute-start(bf16[256,384]{1,0:T(8,128)(2,1)S(1)} %param.68), channel_id=1, source_target_pairs={{0,276},{4,280},{8,284},{12,288},{16,292},{20,296},{24,300},{28,30... | collective-permute-start | bytes 589832 | tf_op jit(solution)/shard_map/cond/branch_68_fun/ppermute | solution.py:376
  62.8 1.3 %copy-start = (bf16[1536,384]{1,0:T(8,128)(2,1)S(1)}, bf16[1536,384]{1,0:T(8,128)(2,1)}, u32[]{:S(2)}) copy-start(bf16[1536,384]{1,0:T(8,128)(2,1)} %wq_hbm.1) | copy-start | bytes 3538948
  64.1 1.3 %copy-start.1 = (bf16[384,1536]{1,0:T(8,128)(2,1)S(1)}, bf16[384,1536]{1,0:T(8,128)(2,1)}, u32[]{:S(2)}) copy-start(bf16[384,1536]{1,0:T(8,128)(2,1)} %wo_hbm.1) | copy-start | bytes 3538948
  65.4 0.7 copy-start.3

commit v2 on v1

v2 whole, which is shorter than its diff:
```python
import functools

import jax
import jax.numpy as jnp
from jax import lax
from jax.experimental import pallas as pl
from jax.experimental.pallas import tpu as pltpu
from jax.sharding import PartitionSpec as P

HEAD_DIM = 64
PAIR = 2 * HEAD_DIM
Y_CHIPS = 8
CHUNK = 128
MESH = pl.DeviceIdType.MESH
F32 = jnp.float32
BF16 = jnp.bfloat16


def attention_kernel(
    seq_count,
    rows,
    owners,
    owner_slot,
    counts,
    act_hbm,
    stale_hbm,
    wq_hbm,
    wo_hbm,
    out,
    act,
    moving,
    landing,
    xg,
    stale,
    wq,
    wo,
    stage,
    pool,
    pool_wide,
    kcat,
    vaug,
    q_s,
    fine_s,
    att_s,
    p_opp,
    p_right,
    p_left,
    p_own,
    in_opp_left,
    in_opp_right,
    in_left,
    in_right,
    load_sem,
    home_send,
    home_recv,
    move_send,
    move_recv,
    x_send,
    x_recv,
    rs_send,
    rs_recv,
    pool_send,
    pool_recv,
):
    width = xg.shape[2]
    total = xg.shape[1]
    chunks = total // CHUNK
    half = CHUNK // 2
    pairs = width // PAIR
    per_window = rows // CHUNK
    z_chips = seq_count // (2 * Y_CHIPS)
    seq = lax.axis_index("seq")
    head = lax.axis_index("head")
    heads = lax.axis_size("head")
    core = lax.rem(seq, 2)
    y = lax.rem(lax.div(seq, 2), Y_CHIPS)
    z = lax.div(seq, 2 * Y_CHIPS)
    right = (seq, lax.rem(head + 1, heads))
    left = (seq, lax.rem(head + heads - 1, heads))
    other_core = (seq + 1 - 2 * core, head)
    inner = y + core * (z - y)
    outer = z + core * (y - z)
    inner_step = 2 + core * (2 * Y_CHIPS - 2)
    outer_step = 2 * Y_CHIPS - core * (2 * Y_CHIPS - 2)
    ring = z_chips

    def inner_peer(j):
        return (seq + (lax.rem(inner + j, ring) - inner) * inner_step, head)

    def outer_peer(j):
        return (seq + (lax.rem(outer + j, ring) - outer) * outer_step, head)

    loads = [
        pltpu.make_async_copy(act_hbm, act, load_sem.at[0]),
        pltpu.make_async_copy(stale_hbm, stale, load_sem.at[1]),
        pltpu.make_async_copy(wq_hbm, wq, load_sem.at[2]),
        pltpu.make_async_copy(wo_hbm, wo, load_sem.at[3]),
    ]
    for load in loads:
        load.start()

    bits = seq_count.bit_length() - 1
    y_bits = tuple(range(1, Y_CHIPS.bit_length()))
    z_bits = tuple(range(Y_CHIPS.bit_length(), bits))
    orders = (y_bits + z_bits + (0,), z_bits + y_bits + (0,))
    streams = [(1, orders[0]), (-1, orders[0]), (1, orders[1]), (-1, orders[1])]
    stream_rows = rows // len(streams)

    def at_distance(by):
        return (lax.rem(seq + by + seq_count, seq_count), head)

    barrier = pltpu.get_barrier_semaphore()
    peers = [left, right, other_core]
    peers += [inner_peer(j) for j in range(1, ring)]
    peers += [outer_peer(j) for j in range(1, ring)]
    peers += [at_distance(1 << k) for k in range(bits)]
    peers += [at_distance(-(1 << k)) for k in range(bits - 1)]
    for peer in peers:
        pl.semaphore_signal(barrier, inc=1, device_id=peer, device_id_type=MESH)
    loads[0].wait()
    in_order = jnp.where(owner_slot[0] == 0, 1.0, 0.0).astype(F32)
    owner_1 = jnp.where(owner_slot[0] == 0, owners[1], owners[0])
    offset = lax.rem(owner_1 - seq + seq_count, seq_count)
    lower, upper = act[0:rows, :].astype(F32), act[rows:, :].astype(F32)
    moving[0:rows, :] = (lower * in_order + upper * (1.0 - in_order)).astype(BF16)
    moving[rows:, :] = (upper * in_order + lower * (1.0 - in_order)).astype(BF16)
    pl.semaphore_wait(barrier, len(peers))

    def remote(src, dst, send, recv, peer):
        return pltpu.make_async_remote_copy(
            src_ref=src,
            dst_ref=dst,
            send_sem=send,
            recv_sem=recv,
            device_id=peer,
            device_id_type=MESH,
        )

    def go_home(c):
        part = pl.ds(c * CHUNK, CHUNK)
        return remote(
            moving.at[part],
            xg.at[0, part],
            home_send.at[c],
            home_recv.at[c],
            at_distance(-1),
        )

    def stride(st, stage):
        sign, order = streams[st]
        if stage == 0:
            src = moving.at[pl.ds(rows + st * stream_rows, stream_rows)]
        else:
            src = landing.at[stage - 1, st]
        return remote(
            src,
            landing.at[stage, st],
            move_send.at[stage, st],
            move_recv.at[stage, st],
            at_distance(sign * (1 << order[stage])),
        )

    def service(stage):
        for st, (sign, order) in enumerate(streams):
            stride(st, stage).wait_recv()
            by = offset if sign > 0 else lax.rem(seq_count - offset, seq_count)
            taking = lax.rem(lax.div(by, 1 << order[stage]), 2).astype(F32)
            if stage == 0:
                kept = moving[pl.ds(rows + st * stream_rows, stream_rows), :]
            else:
                kept = landing[stage - 1, st]
            new = landing[stage, st].astype(F32) * taking + kept.astype(F32) * (1.0 - taking)
            if stage + 1 < bits:
                landing[stage, st] = new.astype(BF16)
                stride(st, stage + 1).start()
            else:
                xg[0, pl.ds(rows + st * stream_rows, stream_rows), :] = new.astype(BF16)

    def direct(c, way):
        peer, slot = ((right, 1), (left, 3))[way]
        part = pl.ds(c * CHUNK, CHUNK)
        return remote(
            xg.at[0, part], xg.at[slot, part], x_send.at[way, c], x_recv.at[way, c], peer
        )

    def forward(c, way):
        peer, slot = ((right, 1), (left, 3))[way]
        part = pl.ds(pl.multiple_of(c * CHUNK + way * half, half), half)
        return remote(
            xg.at[slot, part],
            xg.at[2, part],
            x_send.at[2 + way, c],
            x_recv.at[2 + way, c],
            peer,
        )

    for c in range(per_window):
        go_home(c).start()
    for st in range(len(streams)):
        stride(st, 0).start()

    loads[1].wait()
    stage[...] = jnp.zeros_like(stage)
    row_ids = lax.broadcasted_iota(jnp.int32, (rows, width), 0)
    for kind in range(2):
        for w in range(2):
            count = counts[w]
            part = stale[kind, pl.ds(w * rows, rows), :].astype(F32)
            part = jnp.where(row_ids < count, part, 0.0)
            mean = jnp.sum(part, axis=0, keepdims=True) / count.astype(F32)
            for t in range(pairs):
                at = (kind * 2 + w) * pairs + t
                stage[pl.ds(at, 1), :] = mean[:, t * PAIR : (t + 1) * PAIR]
    pool[core, outer, inner] = stage[...].astype(BF16)

    def inner_copy(j, which):
        ref = pool.at[core, outer, which]
        return remote(ref, ref, pool_send.at[j - 1], pool_recv.at[j - 1], inner_peer(j))

    def outer_copy(j, which):
        ref = pool.at[core, which]
        at = ring + j - 2
        return remote(ref, ref, pool_send.at[at], pool_recv.at[at], outer_peer(j))

    def core_copy(which):
        ref = pool.at[which]
        at = 2 * ring - 2
        return remote(ref, ref, pool_send.at[at], pool_recv.at[at], other_core)

    for j in range(1, ring):
        inner_copy(j, inner).start()

    for c in range(per_window):
        go_home(c).wait_recv()
        for way in range(2):
            direct(c, way).start()
    service(0)

    lanes = lax.broadcasted_iota(jnp.int32, (1, PAIR), 1)
    keep = [
        jnp.where(lanes < HEAD_DIM, 1.0, 0.0),
        jnp.where(lanes < HEAD_DIM, 0.0, 1.0),
    ]

    def lay_out(at, p, key, value):
        for which in range(2):
            part = pl.ds(which * rows, rows)
            kcat[at, p, part, :] = (key * keep[which]).astype(BF16)
            vaug[at, p, part, 0:PAIR] = (value * keep[which]).astype(BF16)
            vaug[at, p, part, PAIR : 2 * PAIR] = jnp.broadcast_to(
                keep[which], (rows, PAIR)
            ).astype(BF16)

    for w in range(2):
        for p in range(pairs):
            cols = slice(p * PAIR, (p + 1) * PAIR)
            lay_out(
                w,
                p,
                stale[0, pl.ds(w * rows, rows), cols].astype(F32),
                stale[1, pl.ds(w * rows, rows), cols].astype(F32),
            )

    def pass_on(c):
        for way in range(2):
            direct(c, way).wait_recv()
            forward(c, way).start()

    def opp_copy(c, way):
        peer = (right, left)[way]
        dst = (in_opp_left, in_opp_right)[way]
        part = pl.ds(way * half, half)
        return remote(
            p_opp.at[c, part], dst.at[c], rs_send.at[way, c], rs_recv.at[way, c], peer
        )

    def share_copy(c, way, piece):
        peer = (right, left)[way]
        src = (p_right, p_left)[way]
        dst = (in_left, in_right)[way]
        part = pl.ds(piece * half, half)
        at = 2 + 2 * way + piece
        return remote(
            src.at[c, part], dst.at[c, part], rs_send.at[at, c], rs_recv.at[at, c], peer
        )

    def relay(c):
        for way in range(2):
            opp_copy(c, way).wait_recv()
            src = (p_right, p_left)[way]
            add = (in_opp_left, in_opp_right)[way]
            part = pl.ds(way * half, half)
            src[c, part, :] = (src[c, part, :].astype(F32) + add[c].astype(F32)).astype(BF16)
            share_copy(c, way, way).start()

    def softmax_out(at, p, query, bias):
        scores = lax.dot_general(
            query, kcat[at, p], (((1,), (1,)), ((), ())), preferred_element_type=F32
        )
        parts = []
        for which in range(2):
            part = scores[:, which * rows : (which + 1) * rows]
            if bias is not None:
                part = part + bias
            top = jnp.max(part, axis=1, keepdims=True)
            parts.append(jnp.exp(part - top).astype(BF16))
        both = jnp.dot(
            jnp.concatenate(parts, axis=1), vaug[at, p], preferred_element_type=F32
        )
        return both[:, 0:PAIR] / both[:, PAIR : 2 * PAIR]

    def project_queries(w):
        here = slice(w * rows, (w + 1) * rows)
        for c in range(w * per_window, (w + 1) * per_window):
            for way in range(2):
                forward(c, way).wait_recv()
        query = None
        for r in range(4):
            source = lax.rem(head + heads - r, heads)
            w_rows = pl.ds(pl.multiple_of(source * width, width), width)
            term = jnp.dot(xg[r, here, :], wq[w_rows, :], preferred_element_type=F32)
            query = term if query is None else query + term
        q_s[here, :] = (query.astype(BF16).astype(F32) * HEAD_DIM ** (-0.5)).astype(BF16)

    slots = lax.broadcasted_iota(jnp.int32, (1, rows), 1)

    def fine_part(w, p, here):
        bias = jnp.where(slots < counts[w], 0.0, -1e30)
        return softmax_out(w, p, q_s[here, p * PAIR : (p + 1) * PAIR], bias)

    def coarse_part(p, here):
        return softmax_out(2, p, q_s[here, p * PAIR : (p + 1) * PAIR], None)

    def project_out(c):
        here = slice(c * CHUNK, (c + 1) * CHUNK)

        def project(r):
            target = lax.rem(head + r, heads)
            cols = pl.ds(pl.multiple_of(target * width, PAIR), width)
            return jnp.dot(
                att_s[here, :], wo[:, cols], preferred_element_type=F32
            ).astype(BF16)

        p_opp[c] = project(2)
        opp_copy(c, 0).start()
        opp_copy(c, 1).start()
        p_right[c] = project(1)
        share_copy(c, 0, 1).start()
        p_left[c] = project(3)
        share_copy(c, 1, 0).start()
        p_own[c] = project(0)

    for j in range(1, ring):
        inner_copy(j, lax.rem(inner + ring - j, ring)).wait_recv()
    for j in range(1, ring):
        outer_copy(j, outer).start()
    service(1)
    pass_on(0)
    pass_on(1)
    service(2)
    for load in loads[2:]:
        load.wait()
    project_queries(0)
    service(3)

    for j in range(1, ring):
        outer_copy(j, lax.rem(outer + ring - j, ring)).wait_recv()
    core_copy(core).start()

    window_0 = slice(0, rows)
    for p in range(pairs):
        fine_s[:, p * PAIR : (p + 1) * PAIR] = fine_part(0, p, window_0)
    service(4)

    core_copy(1 - core).wait_recv()
    for i in range(2):
        for j in range(ring):
            at = (i * ring + j) * ring * 16
            pool_wide[pl.ds(at, ring * 16), :] = (
                pool[i, j].reshape(ring * 16, PAIR).astype(F32)
            )
    for p in range(pairs):
        pooled = []
        for kind in range(2):
            pieces = [
                pool_wide[pl.ds((kind * 2 + w) * pairs + p, seq_count, stride=16), :]
                for w in range(2)
            ]
            pooled.append(jnp.concatenate(pieces, axis=0))
        lay_out(2, p, pooled[0], pooled[1])
    service(5)

    def coarse_chunk(c):
        here = slice(c * CHUNK, (c + 1) * CHUNK)
        for p in range(pairs):
            cols = slice(p * PAIR, (p + 1) * PAIR)
            att_s[here, cols] = (fine_s[here, cols] + coarse_part(p, here)).astype(BF16)
        project_out(c)

    coarse_chunk(0)
    service(6)
    for c in range(per_window, chunks):
        for way in range(2):
            direct(c, way).start()
    coarse_chunk(1)
    relay(0)
    relay(1)
    for c in range(per_window, chunks):
        pass_on(c)
    project_queries(1)
    for c in range(per_window, chunks):
        here = slice(c * CHUNK, (c + 1) * CHUNK)
        for p in range(pairs):
            cols = slice(p * PAIR, (p + 1) * PAIR)
            att_s[here, cols] = (fine_part(1, p, here) + coarse_part(p, here)).astype(BF16)
        project_out(c)
        if c > per_window:
            relay(c - 1)
    relay(chunks - 1)

    def finish(c, carry):
        for way in range(2):
            for piece in range(2):
                share_copy(c, way, piece).wait_recv()
        here = pl.ds(pl.multiple_of(c * CHUNK, CHUNK), CHUNK)
        projected = (
            p_own[c].astype(F32) + in_left[c].astype(F32) + in_right[c].astype(F32)
        )
        out[here, :] = (xg[0, here, :].astype(F32) + projected).astype(BF16)
        return carry

    lax.fori_loop(0, chunks, finish, 0)

    for c in range(per_window):
        go_home(c).wait_send()
    for st in range(len(streams)):
        for at in range(bits):
            stride(st, at).wait_send()
    for c in range(chunks):
        for way in range(2):
            direct(c, way).wait_send()
            forward(c, way).wait_send()
            opp_copy(c, way).wait_send()
            for piece in range(2):
                share_copy(c, way, piece).wait_send()
    for j in range(1, ring):
        inner_copy(j, inner).wait_send()
        outer_copy(j, outer).wait_send()
    core_copy(core).wait_send()


def on_device(activations, owners, owner_slot, counts, stale_pairs, w_query, w_out):
    seq_count = lax.axis_size("seq")
    total, width = activations.shape
    rows = total // owners.shape[0]
    chunks = total // CHUNK
    half = CHUNK // 2
    pairs = width // PAIR
    ring = Y_CHIPS
    bits = seq_count.bit_length() - 1
    hbm = pl.BlockSpec(memory_space=pl.ANY)
    dma = pltpu.SemaphoreType.DMA
    return pl.pallas_call(
        functools.partial(attention_kernel, seq_count, rows),
        out_shape=jax.ShapeDtypeStruct((total, width), BF16),
        in_specs=[pl.BlockSpec(memory_space=pltpu.SMEM)] * 3 + [hbm] * 4,
        out_specs=pl.BlockSpec(memory_space=pltpu.VMEM),
        scratch_shapes=[
            pltpu.VMEM((total, width), BF16),
            pltpu.VMEM((total, width), BF16),
            pltpu.VMEM((bits, 4, rows // 4, width), BF16),
            pltpu.VMEM((4, total, width), BF16),
            pltpu.VMEM(stale_pairs.shape, BF16),
            pltpu.VMEM(w_query.shape, BF16),
            pltpu.VMEM(w_out.shape, BF16),
            pltpu.VMEM((16, PAIR), F32),
            pltpu.VMEM((2, ring, ring, 16, PAIR), BF16),
            pltpu.VMEM((2 * ring * ring * 16, PAIR), F32),
            pltpu.VMEM((3, pairs, 2 * rows, PAIR), BF16),
            pltpu.VMEM((3, pairs, 2 * rows, 2 * PAIR), BF16),
            pltpu.VMEM((total, width), BF16),
            pltpu.VMEM((rows, width), F32),
            pltpu.VMEM((total, width), BF16),
            pltpu.VMEM((chunks, CHUNK, width), BF16),
            pltpu.VMEM((chunks, CHUNK, width), BF16),
            pltpu.VMEM((chunks, CHUNK, width), BF16),
            pltpu.VMEM((chunks, CHUNK, width), BF16),
            pltpu.VMEM((chunks, half, width), BF16),
            pltpu.VMEM((chunks, half, width), BF16),
            pltpu.VMEM((chunks, CHUNK, width), BF16),
            pltpu.VMEM((chunks, CHUNK, width), BF16),
            dma((4,)),
            dma((rows // CHUNK,)),
            dma((rows // CHUNK,)),
            dma((bits, 4)),
            dma((bits, 4)),
            dma((4, chunks)),
            dma((4, chunks)),
            dma((6, chunks)),
            dma((6, chunks)),
            dma((2 * ring - 1,)),
            dma((2 * ring - 1,)),
        ],
        compiler_params=pltpu.CompilerParams(
            collective_id=0, has_side_effects=True, vmem_limit_bytes=60 * 1024 * 1024
        ),
        name="window_attention",
    )(owners, owner_slot, counts, activations, stale_pairs, w_query, w_out)


def solution(mesh):
    placed = (
        P("seq", "head"),
        P("seq"),
        P("seq"),
        P("seq"),
        P(None, "seq", "head"),
        P(None, "head"),
        P("head", None),
    )
    return jax.shard_map(
        on_device, mesh=mesh, in_specs=placed, out_specs=P("seq", "head"), check_vma=False
    )
```

time: 123 us -> 83.7 us (0.68)
  starting transfers between devices: 36.3 us -> 0 us
  Pallas kernels: 55.9 us -> 81.5 us
  waiting for transfers between devices: 21.9 us -> 0 us
  local copies, waits for them, and re-layouts: 5.33 us -> 1.78 us
  between operations: 2.14 us -> 0.01 us
    ppermute x2 -> x0, starting transfers between devices: 36.3 us -> none  [shift(): lax.ppermute(value, 'seq', [(i, (i + by) % seq_count) for i in range(seq_...]
    pallas_call x1, Pallas kernels: 55.9 us -> 81.5 us  [on_device(): pl.pallas_call(functools.partial(attention_kernel, seq_count, rows), out_...]
    ppermute x2 -> x0, waiting for transfers between devices: 21.9 us -> none  [shift(): lax.ppermute(value, 'seq', [(i, (i + by) % seq_count) for i in range(seq_...]
    unnamed x9 -> x1, local copies, waits for them, and re-layouts: 3.95 us -> 1.78 us
    slice x1 -> x0, local copies, waits for them, and re-layouts: 1.38 us -> none  [on_device(): owner_1 = jnp.where(in_order, owners[1], owners[0])]
  transfers between devices with their start and end apart: 2 -> 0, of which waited for: 1 -> 0; matrix products, arithmetic and copies ran while one was open for 1% -> 0% of each run, Pallas kernels for 0% -> 0%
where the time goes in v2:
time: 83.7 us; the launch traced here: 83.3 us
  Pallas kernels  81.5 us (97%)
  local copies, waits for them, and re-layouts  1.78 us (2%)
    pallas_call x1, Pallas kernels, on_device(): pl.pallas_call(functools.partial(attention_kernel, seq_count, rows), out_...  81.5 us
    unnamed x1, local copies, waits for them, and re-layouts  1.78 us

profile of v2, /device:TPU:1, one launch (start us, length us, event | category | flops | bytes accessed | tf_op | source)
XLA Modules:
  0.0 83.3 jit_solution(17271489947395065474)
XLA Ops:
  0.0 81.5 %window_attention.1 = bf16[512,384]{1,0:T(8,128)(2,1)} custom-call(s32[2]{0:T(128)} %owners.1, s32[2]{0:T(128)} %owner_slot.1, s32[2]{0:T(128)} %counts.1, bf16[512,384]{1,0:T(8,128)(2,1)} %act_hbm.1, bf16[2,512,384]{2,1,0:T(8,128)(2,1)} %stale_hbm.1, bf16[1536,384]{1,0:T(8,128)(2,1)} %wq_hbm.1, bf16[384,1536]{1,0:T(8,128)(2,1)} %wo_hbm.1), custom_call_target="tpu_custom_call" | custom-call | tf_op jit(solution)/shard_map/window_attention/pallas_call | solution.py:463
  81.5 1.8 %copy.9 = bf16[512,384]{1,0:T(8,128)(2,1)} copy(bf16[512,384]{1,0:T(8,128)(2,1)} %window_attention.1) | data formatting | bytes 786432

commit v3 on v2

--- a/solution.py
+++ b/solution.py
@@ -99,12 +99,10 @@
     for load in loads:
         load.start()
 
-    bits = seq_count.bit_length() - 1
-    y_bits = tuple(range(1, Y_CHIPS.bit_length()))
-    z_bits = tuple(range(Y_CHIPS.bit_length(), bits))
-    orders = (y_bits + z_bits + (0,), z_bits + y_bits + (0,))
-    streams = [(1, orders[0]), (-1, orders[0]), (1, orders[1]), (-1, orders[1])]
-    stream_rows = rows // len(streams)
+    plane = 2 * Y_CHIPS
+    orders = ((2, 6, plane, 3 * plane, 1), (plane, 3 * plane, 2, 6, 1))
+    stages = len(orders[0])
+    stream_rows = CHUNK // 2
 
     def at_distance(by):
         return (lax.rem(seq + by + seq_count, seq_count), head)
@@ -113,14 +111,22 @@
     peers = [left, right, other_core]
     peers += [inner_peer(j) for j in range(1, ring)]
     peers += [outer_peer(j) for j in range(1, ring)]
-    peers += [at_distance(1 << k) for k in range(bits)]
-    peers += [at_distance(-(1 << k)) for k in range(bits - 1)]
+    peers += [at_distance(sign * by) for by in orders[0] for sign in (1, -1)]
     for peer in peers:
         pl.semaphore_signal(barrier, inc=1, device_id=peer, device_id_type=MESH)
     loads[0].wait()
     in_order = jnp.where(owner_slot[0] == 0, 1.0, 0.0).astype(F32)
     owner_1 = jnp.where(owner_slot[0] == 0, owners[1], owners[0])
     offset = lax.rem(owner_1 - seq + seq_count, seq_count)
+    y_part = lax.rem(lax.div(offset, 2) + 4, ring)
+    z_part = lax.rem(lax.div(offset + ring, plane) + 4, ring)
+    digits = {
+        1: lax.rem(offset, 2),
+        2: lax.rem(y_part, 3) - 1,
+        6: lax.div(y_part, 3) - 1,
+        plane: lax.rem(z_part, 3) - 1,
+        3 * plane: lax.div(z_part, 3) - 1,
+    }
     lower, upper = act[0:rows, :].astype(F32), act[rows:, :].astype(F32)
     moving[0:rows, :] = (lower * in_order + upper * (1.0 - in_order)).astype(BF16)
     moving[rows:, :] = (upper * in_order + lower * (1.0 - in_order)).astype(BF16)
@@ -146,35 +152,46 @@
             at_distance(-1),
         )
 
-    def stride(st, stage):
-        sign, order = streams[st]
+    def first_row(g, st):
+        return rows + g * CHUNK + st * stream_rows
+
+    def ways(stage):
+        return 1 if orders[0][stage] == 1 else 2
+
+    def stride(stage, g, st, way):
         if stage == 0:
-            src = moving.at[pl.ds(rows + st * stream_rows, stream_rows)]
+            src = moving.at[pl.ds(first_row(g, st), stream_rows)]
         else:
-            src = landing.at[stage - 1, st]
+            src = landing.at[stage - 1, g, st, 0]
         return remote(
             src,
-            landing.at[stage, st],
-            move_send.at[stage, st],
-            move_recv.at[stage, st],
-            at_distance(sign * (1 << order[stage])),
-        )
-
-    def service(stage):
-        for st, (sign, order) in enumerate(streams):
-            stride(st, stage).wait_recv()
-            by = offset if sign > 0 else lax.rem(seq_count - offset, seq_count)
-            taking = lax.rem(lax.div(by, 1 << order[stage]), 2).astype(F32)
+            landing.at[stage, g, st, way],
+            move_send.at[stage, g, st, way],
+            move_recv.at[stage, g, st, way],
+            at_distance((1 - 2 * way) * orders[st][stage]),
+        )
+
+    def service(stage, g):
+        for st in range(2):
+            digit = digits[orders[st][stage]]
             if stage == 0:
-                kept = moving[pl.ds(rows + st * stream_rows, stream_rows), :]
+                new = moving[pl.ds(first_row(g, st), stream_rows), :].astype(F32)
             else:
-                kept = landing[stage - 1, st]
-            new = landing[stage, st].astype(F32) * taking + kept.astype(F32) * (1.0 - taking)
-            if stage + 1 < bits:
-                landing[stage, st] = new.astype(BF16)
-                stride(st, stage + 1).start()
+                new = landing[stage - 1, g, st, 0].astype(F32)
+            new = new * (digit == 0).astype(F32)
+            for way in range(ways(stage)):
+                stride(stage, g, st, way).wait_recv()
+                taking = (digit == 1 - 2 * way).astype(F32)
+                new = new + landing[stage, g, st, way].astype(F32) * taking
+            if stage + 1 < stages:
+                landing[stage, g, st, 0] = new.astype(BF16)
+                for way in range(ways(stage + 1)):
+                    stride(stage + 1, g, st, way).start()
             else:
-                xg[0, pl.ds(rows + st * stream_rows, stream_rows), :] = new.astype(BF16)
+                xg[0, pl.ds(first_row(g, st), stream_rows), :] = new.astype(BF16)
+        if stage + 1 == stages:
+            for way in range(2):
+                direct(per_window + g, way).start()
 
     def direct(c, way):
         peer, slot = ((right, 1), (left, 3))[way]
@@ -196,8 +213,10 @@
 
     for c in range(per_window):
         go_home(c).start()
-    for st in range(len(streams)):
-        stride(st, 0).start()
+    for g in range(per_window):
+        for st in range(2):
+            for way in range(2):
+                stride(0, g, st, way).start()
 
     loads[1].wait()
     stage[...] = jnp.zeros_like(stage)
@@ -234,7 +253,8 @@
         go_home(c).wait_recv()
         for way in range(2):
             direct(c, way).start()
-    service(0)
+    service(0, 0)
+    service(0, 1)
 
     lanes = lax.broadcasted_iota(jnp.int32, (1, PAIR), 1)
     keep = [
@@ -245,7 +265,7 @@
     def lay_out(at, p, key, value):
         for which in range(2):
             part = pl.ds(which * rows, rows)
-            kcat[at, p, part, :] = (key * keep[which]).astype(BF16)
+            kcat[at, p, :, part] = jnp.transpose(key * keep[which]).astype(BF16)
             vaug[at, p, part, 0:PAIR] = (value * keep[which]).astype(BF16)
             vaug[at, p, part, PAIR : 2 * PAIR] = jnp.broadcast_to(
                 keep[which], (rows, PAIR)
@@ -294,9 +314,7 @@
             share_copy(c, way, way).start()
 
     def softmax_out(at, p, query, bias):
-        scores = lax.dot_general(
-            query, kcat[at, p], (((1,), (1,)), ((), ())), preferred_element_type=F32
-        )
+        scores = jnp.dot(query, kcat[at, p], preferred_element_type=F32)
         parts = []
         for which in range(2):
             part = scores[:, which * rows : (which + 1) * rows]
@@ -309,9 +327,9 @@
         )
         return both[:, 0:PAIR] / both[:, PAIR : 2 * PAIR]
 
-    def project_queries(w):
-        here = slice(w * rows, (w + 1) * rows)
-        for c in range(w * per_window, (w + 1) * per_window):
+    def project_queries(first_chunk, count):
+        here = slice(first_chunk * CHUNK, (first_chunk + count) * CHUNK)
+        for c in range(first_chunk, first_chunk + count):
             for way in range(2):
                 forward(c, way).wait_recv()
         query = None
@@ -350,27 +368,47 @@
         share_copy(c, 1, 0).start()
         p_own[c] = project(0)
 
+    def fine_chunk(p):
+        fine_s[:, p * PAIR : (p + 1) * PAIR] = fine_part(0, p, slice(0, rows))
+
+    def coarse_chunk(c):
+        here = slice(c * CHUNK, (c + 1) * CHUNK)
+        for p in range(pairs):
+            cols = slice(p * PAIR, (p + 1) * PAIR)
+            att_s[here, cols] = (fine_s[here, cols] + coarse_part(p, here)).astype(BF16)
+        project_out(c)
+
+    def whole_chunk(c):
+        project_queries(c, 1)
+        here = slice(c * CHUNK, (c + 1) * CHUNK)
+        for p in range(pairs):
+            cols = slice(p * PAIR, (p + 1) * PAIR)
+            att_s[here, cols] = (fine_part(1, p, here) + coarse_part(p, here)).astype(BF16)
+        project_out(c)
+
     for j in range(1, ring):
         inner_copy(j, lax.rem(inner + ring - j, ring)).wait_recv()
     for j in range(1, ring):
         outer_copy(j, outer).start()
-    service(1)
+    service(1, 0)
     pass_on(0)
+    service(1, 1)
     pass_on(1)
-    service(2)
-    for load in loads[2:]:
-        load.wait()
-    project_queries(0)
-    service(3)
-
+    service(2, 0)
     for j in range(1, ring):
         outer_copy(j, lax.rem(outer + ring - j, ring)).wait_recv()
     core_copy(core).start()
-
-    window_0 = slice(0, rows)
-    for p in range(pairs):
-        fine_s[:, p * PAIR : (p + 1) * PAIR] = fine_part(0, p, window_0)
-    service(4)
+    service(2, 1)
+    for load in loads[2:]:
+        load.wait()
+    project_queries(0, 2)
+    service(3, 0)
+    fine_chunk(0)
+    service(3, 1)
+    fine_chunk(1)
+    service(4, 0)
+    fine_chunk(2)
+    service(4, 1)
 
     core_copy(1 - core).wait_recv()
     for i in range(2):
@@ -388,35 +426,17 @@
             ]
             pooled.append(jnp.concatenate(pieces, axis=0))
         lay_out(2, p, pooled[0], pooled[1])
-    service(5)
-
-    def coarse_chunk(c):
-        here = slice(c * CHUNK, (c + 1) * CHUNK)
-        for p in range(pairs):
-            cols = slice(p * PAIR, (p + 1) * PAIR)
-            att_s[here, cols] = (fine_s[here, cols] + coarse_part(p, here)).astype(BF16)
-        project_out(c)
 
     coarse_chunk(0)
-    service(6)
-    for c in range(per_window, chunks):
-        for way in range(2):
-            direct(c, way).start()
+    pass_on(2)
     coarse_chunk(1)
+    pass_on(3)
     relay(0)
+    whole_chunk(2)
     relay(1)
-    for c in range(per_window, chunks):
-        pass_on(c)
-    project_queries(1)
-    for c in range(per_window, chunks):
-        here = slice(c * CHUNK, (c + 1) * CHUNK)
-        for p in range(pairs):
-            cols = slice(p * PAIR, (p + 1) * PAIR)
-            att_s[here, cols] = (fine_part(1, p, here) + coarse_part(p, here)).astype(BF16)
-        project_out(c)
-        if c > per_window:
-            relay(c - 1)
-    relay(chunks - 1)
+    whole_chunk(3)
+    relay(2)
+    relay(3)
 
     def finish(c, carry):
         for way in range(2):
@@ -433,9 +453,11 @@
 
     for c in range(per_window):
         go_home(c).wait_send()
-    for st in range(len(streams)):
-        for at in range(bits):
-            stride(st, at).wait_send()
+    for stage_at in range(stages):
+        for g in range(per_window):
+            for st in range(2):
+                for way in range(ways(stage_at)):
+                    stride(stage_at, g, st, way).wait_send()
     for c in range(chunks):
         for way in range(2):
             direct(c, way).wait_send()
@@ -457,7 +479,7 @@
     half = CHUNK // 2
     pairs = width // PAIR
     ring = Y_CHIPS
-    bits = seq_count.bit_length() - 1
+    groups = rows // CHUNK
     hbm = pl.BlockSpec(memory_space=pl.ANY)
     dma = pltpu.SemaphoreType.DMA
     return pl.pallas_call(
@@ -468,7 +490,7 @@
         scratch_shapes=[
             pltpu.VMEM((total, width), BF16),
             pltpu.VMEM((total, width), BF16),
-            pltpu.VMEM((bits, 4, rows // 4, width), BF16),
+            pltpu.VMEM((5, groups, 2, 2, CHUNK // 2, width), BF16),
             pltpu.VMEM((4, total, width), BF16),
             pltpu.VMEM(stale_pairs.shape, BF16),
             pltpu.VMEM(w_query.shape, BF16),
@@ -476,7 +498,7 @@
             pltpu.VMEM((16, PAIR), F32),
             pltpu.VMEM((2, ring, ring, 16, PAIR), BF16),
             pltpu.VMEM((2 * ring * ring * 16, PAIR), F32),
-            pltpu.VMEM((3, pairs, 2 * rows, PAIR), BF16),
+            pltpu.VMEM((3, pairs, PAIR, 2 * rows), BF16),
             pltpu.VMEM((3, pairs, 2 * rows, 2 * PAIR), BF16),
             pltpu.VMEM((total, width), BF16),
             pltpu.VMEM((rows, width), F32),
@@ -492,8 +514,8 @@
             dma((4,)),
             dma((rows // CHUNK,)),
             dma((rows // CHUNK,)),
-            dma((bits, 4)),
-            dma((bits, 4)),
+            dma((5, groups, 2, 2)),
+            dma((5, groups, 2, 2)),
             dma((4, chunks)),
             dma((4, chunks)),
             dma((6, chunks)),

time: 83.7 us -> 76.5 us (0.914); the launches traced: 83.3 us -> 75.2 us
  Pallas kernels: 81.5 us -> 73.4 us
    pallas_call x1, Pallas kernels: 81.5 us -> 73.4 us  [on_device(): pl.pallas_call(functools.partial(attention_kernel, seq_count, rows), out_...]
where the time goes in v3:
time: 76.5 us; the launch traced here: 75.2 us
  Pallas kernels  73.4 us (96%)
  local copies, waits for them, and re-layouts  1.78 us (2%)
    pallas_call x1, Pallas kernels, on_device(): pl.pallas_call(functools.partial(attention_kernel, seq_count, rows), out_...  73.4 us
    unnamed x1, local copies, waits for them, and re-layouts  1.78 us

profile of v3, /device:TPU:1, one launch (start us, length us, event | category | flops | bytes accessed | tf_op | source)
XLA Modules:
  0.0 75.2 jit_solution(4010211678822052359)
XLA Ops:
  0.0 73.4 %window_attention.1 = bf16[512,384]{1,0:T(8,128)(2,1)} custom-call(s32[2]{0:T(128)} %owners.1, s32[2]{0:T(128)} %owner_slot.1, s32[2]{0:T(128)} %counts.1, bf16[512,384]{1,0:T(8,128)(2,1)} %act_hbm.1, bf16[2,512,384]{2,1,0:T(8,128)(2,1)} %stale_hbm.1, bf16[1536,384]{1,0:T(8,128)(2,1)} %wq_hbm.1, bf16[384,1536]{1,0:T(8,128)(2,1)} %wo_hbm.1), custom_call_target="tpu_custom_call" | custom-call | tf_op jit(solution)/shard_map/window_attention/pallas_call | solution.py:485
  73.4 1.8 %copy.9 = bf16[512,384]{1,0:T(8,128)(2,1)} copy(bf16[512,384]{1,0:T(8,128)(2,1)} %window_attention.1) | data formatting | bytes 786432

commit v4 on v3

v4 whole, which is shorter than its diff:
```python
import functools

import jax
import jax.numpy as jnp
from jax import lax
from jax.experimental import pallas as pl
from jax.experimental.pallas import tpu as pltpu
from jax.sharding import PartitionSpec as P

HEAD_DIM = 64
PAIR = 2 * HEAD_DIM
Y_CHIPS = 8
CHUNK = 128
MESH = pl.DeviceIdType.MESH
F32 = jnp.float32
BF16 = jnp.bfloat16


def attention_kernel(
    seq_count,
    rows,
    chunks,
    owners,
    owner_slot,
    counts,
    act_hbm,
    stale_hbm,
    wq_hbm,
    wo_hbm,
    out,
    act,
    moving,
    landing,
    xg,
    stale,
    wq,
    wo,
    stage,
    pool,
    pool_wide,
    kcat,
    vaug,
    q_s,
    att_s,
    p_opp,
    p_right,
    p_left,
    p_own,
    in_opp_left,
    in_opp_right,
    in_left,
    in_right,
    load_sem,
    home_send,
    home_recv,
    move_send,
    move_recv,
    x_send,
    x_recv,
    rs_send,
    rs_recv,
    pool_send,
    pool_recv,
):
    width = xg.shape[2]
    total = xg.shape[1]
    pairs = width // PAIR
    z_chips = seq_count // (2 * Y_CHIPS)
    seq = lax.axis_index("seq")
    head = lax.axis_index("head")
    heads = lax.axis_size("head")
    core = lax.rem(seq, 2)
    y = lax.rem(lax.div(seq, 2), Y_CHIPS)
    z = lax.div(seq, 2 * Y_CHIPS)
    right = (seq, lax.rem(head + 1, heads))
    left = (seq, lax.rem(head + heads - 1, heads))
    other_core = (seq + 1 - 2 * core, head)
    inner = y + core * (z - y)
    outer = z + core * (y - z)
    inner_step = 2 + core * (2 * Y_CHIPS - 2)
    outer_step = 2 * Y_CHIPS - core * (2 * Y_CHIPS - 2)
    ring = z_chips

    def inner_peer(j):
        return (seq + (lax.rem(inner + j, ring) - inner) * inner_step, head)

    def outer_peer(j):
        return (seq + (lax.rem(outer + j, ring) - outer) * outer_step, head)

    loads = [
        pltpu.make_async_copy(act_hbm, act, load_sem.at[0]),
        pltpu.make_async_copy(stale_hbm, stale, load_sem.at[1]),
        pltpu.make_async_copy(wq_hbm, wq, load_sem.at[2]),
        pltpu.make_async_copy(wo_hbm, wo, load_sem.at[3]),
    ]
    for load in loads:
        load.start()

    plane = 2 * Y_CHIPS
    orders = ((1, 2, 6, plane, 3 * plane), (1, plane, 3 * plane, 2, 6))
    stages = len(orders[0])
    stream_rows = CHUNK // 2

    def at_distance(by):
        return (lax.rem(seq + by + seq_count, seq_count), head)

    barrier = pltpu.get_barrier_semaphore()
    peers = [left, right, other_core]
    peers += [inner_peer(j) for j in range(1, ring)]
    peers += [outer_peer(j) for j in range(1, ring)]
    peers += [at_distance(sign * by) for by in orders[0] for sign in (1, -1)]
    for peer in peers:
        pl.semaphore_signal(barrier, inc=1, device_id=peer, device_id_type=MESH)
    loads[0].wait()
    in_order = jnp.where(owner_slot[0] == 0, 1.0, 0.0).astype(F32)
    owner_1 = jnp.where(owner_slot[0] == 0, owners[1], owners[0])
    offset = lax.rem(owner_1 - seq + seq_count, seq_count)
    y_part = lax.rem(lax.div(offset, 2) + 4, ring)
    z_part = lax.rem(lax.div(offset + ring, plane) + 4, ring)
    digits = {
        1: lax.rem(offset, 2),
        2: lax.rem(y_part, 3) - 1,
        6: lax.div(y_part, 3) - 1,
        plane: lax.rem(z_part, 3) - 1,
        3 * plane: lax.div(z_part, 3) - 1,
    }
    lower, upper = act[0:rows, :].astype(F32), act[rows:, :].astype(F32)
    moving[0:rows, :] = (lower * in_order + upper * (1.0 - in_order)).astype(BF16)
    moving[rows:, :] = (upper * in_order + lower * (1.0 - in_order)).astype(BF16)
    pl.semaphore_wait(barrier, len(peers))

    def remote(src, dst, send, recv, peer):
        return pltpu.make_async_remote_copy(
            src_ref=src,
            dst_ref=dst,
            send_sem=send,
            recv_sem=recv,
            device_id=peer,
            device_id_type=MESH,
        )

    go_home = remote(
        moving.at[pl.ds(0, rows)],
        xg.at[0, pl.ds(0, rows)],
        home_send.at[0],
        home_recv.at[0],
        at_distance(-1),
    )

    groups = len(chunks) - 1

    def all_of(c):
        start, size = chunks[c]
        return pl.ds(start, size)

    def half_of(c, piece):
        start, size = chunks[c]
        return pl.ds(start + piece * size // 2, size // 2)

    def first_row(g, st):
        return chunks[1 + g][0] + st * stream_rows

    def ways(stage):
        return 1 if orders[0][stage] == 1 else 2

    def stride(stage, g, st, way):
        if stage == 0:
            src = moving.at[pl.ds(first_row(g, st), stream_rows)]
        else:
            src = landing.at[stage - 1, g, st, 0]
        return remote(
            src,
            landing.at[stage, g, st, way],
            move_send.at[stage, g, st, way],
            move_recv.at[stage, g, st, way],
            at_distance((1 - 2 * way) * orders[st][stage]),
        )

    def service(stage, g):
        for st in range(2):
            digit = digits[orders[st][stage]]
            if stage == 0:
                new = moving[pl.ds(first_row(g, st), stream_rows), :].astype(F32)
            else:
                new = landing[stage - 1, g, st, 0].astype(F32)
            new = new * (digit == 0).astype(F32)
            for way in range(ways(stage)):
                stride(stage, g, st, way).wait_recv()
                taking = (digit == 1 - 2 * way).astype(F32)
                new = new + landing[stage, g, st, way].astype(F32) * taking
            if stage + 1 < stages:
                landing[stage, g, st, 0] = new.astype(BF16)
                for way in range(ways(stage + 1)):
                    stride(stage + 1, g, st, way).start()
            else:
                xg[0, pl.ds(first_row(g, st), stream_rows), :] = new.astype(BF16)
        if stage + 1 == stages:
            for way in range(2):
                direct(1 + g, way).start()

    def direct(c, way):
        peer, slot = ((right, 1), (left, 3))[way]
        part = all_of(c)
        return remote(
            xg.at[0, part], xg.at[slot, part], x_send.at[way, c], x_recv.at[way, c], peer
        )

    def forward(c, way):
        peer, slot = ((right, 1), (left, 3))[way]
        part = half_of(c, way)
        return remote(
            xg.at[slot, part],
            xg.at[2, part],
            x_send.at[2 + way, c],
            x_recv.at[2 + way, c],
            peer,
        )

    for g in range(groups):
        for st in range(2):
            for way in range(ways(0)):
                stride(0, g, st, way).start()
    go_home.start()

    loads[1].wait()
    stage[...] = jnp.zeros_like(stage)
    row_ids = lax.broadcasted_iota(jnp.int32, (rows, width), 0)
    for kind in range(2):
        for w in range(2):
            count = counts[w]
            part = stale[kind, pl.ds(w * rows, rows), :].astype(F32)
            part = jnp.where(row_ids < count, part, 0.0)
            mean = jnp.sum(part, axis=0, keepdims=True) / count.astype(F32)
            for t in range(pairs):
                at = (kind * 2 + w) * pairs + t
                stage[pl.ds(at, 1), :] = mean[:, t * PAIR : (t + 1) * PAIR]
    pool[core, outer, inner] = stage[...].astype(BF16)

    def inner_copy(j, which):
        ref = pool.at[core, outer, which]
        return remote(ref, ref, pool_send.at[j - 1], pool_recv.at[j - 1], inner_peer(j))

    def outer_copy(j, which):
        ref = pool.at[core, which]
        at = ring + j - 2
        return remote(ref, ref, pool_send.at[at], pool_recv.at[at], outer_peer(j))

    def core_copy(which):
        ref = pool.at[which]
        at = 2 * ring - 2
        return remote(ref, ref, pool_send.at[at], pool_recv.at[at], other_core)

    for j in range(1, ring):
        inner_copy(j, inner).start()

    for g in range(groups):
        service(0, g)
    go_home.wait_recv()
    for way in range(2):
        direct(0, way).start()

    def lay_out(at, p, key, value):
        kcat[at, p] = jnp.transpose(key).astype(BF16)
        vaug[at, p, :, 0:PAIR] = value
        vaug[at, p, :, PAIR : 2 * PAIR] = jnp.ones((rows, PAIR), BF16)

    for w in range(2):
        for p in range(pairs):
            cols = slice(p * PAIR, (p + 1) * PAIR)
            lay_out(
                w,
                p,
                stale[0, pl.ds(w * rows, rows), cols].astype(F32),
                stale[1, pl.ds(w * rows, rows), cols],
            )

    def pass_on(c):
        for way in range(2):
            direct(c, way).wait_recv()
            forward(c, way).start()

    def opp_copy(c, way):
        peer = (right, left)[way]
        dst = (in_opp_left, in_opp_right)[way]
        part = half_of(c, way)
        return remote(
            p_opp.at[part], dst.at[part], rs_send.at[way, c], rs_recv.at[way, c], peer
        )

    def share_copy(c, way, piece):
        peer = (right, left)[way]
        src = (p_right, p_left)[way]
        dst = (in_left, in_right)[way]
        part = half_of(c, piece)
        at = 2 + 2 * way + piece
        return remote(
            src.at[part], dst.at[part], rs_send.at[at, c], rs_recv.at[at, c], peer
        )

    def relay(c):
        for way in range(2):
            opp_copy(c, way).wait_recv()
            src = (p_right, p_left)[way]
            add = (in_opp_left, in_opp_right)[way]
            part = half_of(c, way)
            src[part, :] = (src[part, :].astype(F32) + add[part, :].astype(F32)).astype(BF16)
            share_copy(c, way, way).start()

    lanes = lax.broadcasted_iota(jnp.int32, (1, width), 1)
    of_first = lax.rem(lanes, PAIR) < HEAD_DIM

    def project_queries(c):
        for way in range(2):
            forward(c, way).wait_recv()
        here = all_of(c)
        query = None
        for r in range(4):
            source = lax.rem(head + heads - r, heads)
            w_rows = pl.ds(pl.multiple_of(source * width, width), width)
            term = jnp.dot(xg[r, here, :], wq[w_rows, :], preferred_element_type=F32)
            query = term if query is None else query + term
        query = query.astype(BF16).astype(F32) * HEAD_DIM ** (-0.5)
        q_s[0, here, :] = jnp.where(of_first, query, 0.0).astype(BF16)
        q_s[1, here, :] = jnp.where(of_first, 0.0, query).astype(BF16)

    slots = lax.broadcasted_iota(jnp.int32, (1, rows), 1)
    biases = [jnp.where(slots < counts[w], 0.0, -1e30) for w in range(2)]

    def softmax_out(at, p, query, bias):
        size = query.shape[0] // 2
        scores = jnp.dot(query, kcat[at, p], preferred_element_type=F32)
        if bias is not None:
            scores = scores + bias
        top = jnp.max(scores, axis=1, keepdims=True)
        weights = jnp.exp(scores - top).astype(BF16)
        both = jnp.dot(weights, vaug[at, p], preferred_element_type=F32)
        pick = of_first[:, 0:PAIR]
        summed = jnp.where(pick, both[0:size, 0:PAIR], both[size:, 0:PAIR])
        mass = jnp.where(pick, both[0:size, PAIR:], both[size:, PAIR:])
        return summed / mass

    def attend(c, w, p):
        here = all_of(c)
        cols = slice(p * PAIR, (p + 1) * PAIR)
        query = jnp.concatenate([q_s[0, here, cols], q_s[1, here, cols]], axis=0)
        fine = softmax_out(w, p, query, biases[w])
        coarse = softmax_out(2, p, query, None)
        att_s[here, cols] = (fine + coarse).astype(BF16)

    def project(c, r):
        target = lax.rem(head + r, heads)
        cols = pl.ds(pl.multiple_of(target * width, PAIR), width)
        return jnp.dot(
            att_s[all_of(c), :], wo[:, cols], preferred_element_type=F32
        ).astype(BF16)

    def project_out(c):
        p_opp[all_of(c), :] = project(c, 2)
        opp_copy(c, 0).start()
        opp_copy(c, 1).start()
        p_right[all_of(c), :] = project(c, 1)
        share_copy(c, 0, 1).start()
        p_left[all_of(c), :] = project(c, 3)
        share_copy(c, 1, 0).start()

    def project_own(c):
        p_own[all_of(c), :] = project(c, 0)

    def finish(c):
        for way in range(2):
            for piece in range(2):
                share_copy(c, way, piece).wait_recv()
        here = all_of(c)
        projected = (
            p_own[here, :].astype(F32)
            + in_left[here, :].astype(F32)
            + in_right[here, :].astype(F32)
        )
        out[here, :] = (xg[0, here, :].astype(F32) + projected).astype(BF16)

    for j in range(1, ring):
        inner_copy(j, lax.rem(inner + ring - j, ring)).wait_recv()
    for j in range(1, ring):
        outer_copy(j, outer).start()
    service(1, 0)
    service(1, 1)
    pass_on(0)
    service(2, 0)
    service(2, 1)
    for j in range(1, ring):
        outer_copy(j, lax.rem(outer + ring - j, ring)).wait_recv()
    core_copy(core).start()
    service(3, 0)
    service(3, 1)
    for load in loads[2:]:
        load.wait()
    project_queries(0)
    service(4, 0)
    service(4, 1)

    core_copy(1 - core).wait_recv()
    for i in range(2):
        for j in range(ring):
            at = (i * ring + j) * ring * 16
            pool_wide[pl.ds(at, ring * 16), :] = (
                pool[i, j].reshape(ring * 16, PAIR).astype(F32)
            )
    for p in range(pairs):
        pooled = []
        for kind in range(2):
            pieces = [
                pool_wide[pl.ds((kind * 2 + w) * pairs + p, seq_count, stride=16), :]
                for w in range(2)
            ]
            pooled.append(jnp.concatenate(pieces, axis=0))
        lay_out(2, p, pooled[0], pooled[1].astype(BF16))

    attend(0, 0, 0)
    pass_on(1)
    attend(0, 0, 1)
    pass_on(2)
    attend(0, 0, 2)
    project_out(0)

    project_queries(1)
    for p in range(pairs):
        attend(1, 1, p)
    project_out(1)
    relay(0)
    project_queries(2)
    for p in range(pairs):
        attend(2, 1, p)
    project_out(2)
    relay(1)
    for c in range(3):
        project_own(c)
    finish(0)
    relay(2)

    for j in range(1, ring):
        inner_copy(j, inner).wait_send()
        outer_copy(j, outer).wait_send()
    core_copy(core).wait_send()
    go_home.wait_send()
    for step in range(stages - 1):
        for g in range(groups):
            for st in range(2):
                for way in range(ways(step)):
                    stride(step, g, st, way).wait_send()
    for way in range(2):
        direct(0, way).wait_send()
        forward(0, way).wait_send()

    for g in range(groups):
        for st in range(2):
            for way in range(ways(stages - 1)):
                stride(stages - 1, g, st, way).wait_send()
    for c in range(1, len(chunks)):
        for way in range(2):
            direct(c, way).wait_send()
            forward(c, way).wait_send()
    finish(1)
    finish(2)
    for c in range(len(chunks)):
        for way in range(2):
            opp_copy(c, way).wait_send()
            for piece in range(2):
                share_copy(c, way, piece).wait_send()


def on_device(activations, owners, owner_slot, counts, stale_pairs, w_query, w_out):
    seq_count = lax.axis_size("seq")
    total, width = activations.shape
    rows = total // owners.shape[0]
    pairs = width // PAIR
    ring = Y_CHIPS
    chunks = [(0, rows)] + [(at, CHUNK) for at in range(rows, total, CHUNK)]
    groups = len(chunks) - 1
    hbm = pl.BlockSpec(memory_space=pl.ANY)
    dma = pltpu.SemaphoreType.DMA
    return pl.pallas_call(
        functools.partial(attention_kernel, seq_count, rows, chunks),
        out_shape=jax.ShapeDtypeStruct((total, width), BF16),
        in_specs=[pl.BlockSpec(memory_space=pltpu.SMEM)] * 3 + [hbm] * 4,
        out_specs=pl.BlockSpec(memory_space=pltpu.VMEM),
        scratch_shapes=[
            pltpu.VMEM((total, width), BF16),
            pltpu.VMEM((total, width), BF16),
            pltpu.VMEM((5, groups, 2, 2, CHUNK // 2, width), BF16),
            pltpu.VMEM((4, total, width), BF16),
            pltpu.VMEM(stale_pairs.shape, BF16),
            pltpu.VMEM(w_query.shape, BF16),
            pltpu.VMEM(w_out.shape, BF16),
            pltpu.VMEM((16, PAIR), F32),
            pltpu.VMEM((2, ring, ring, 16, PAIR), BF16),
            pltpu.VMEM((2 * ring * ring * 16, PAIR), F32),
            pltpu.VMEM((3, pairs, PAIR, rows), BF16),
            pltpu.VMEM((3, pairs, rows, 2 * PAIR), BF16),
            pltpu.VMEM((2, total, width), BF16),
        ]
        + [pltpu.VMEM((total, width), BF16)] * 9
        + [
            dma((4,)),
            dma((1,)),
            dma((1,)),
            dma((5, groups, 2, 2)),
            dma((5, groups, 2, 2)),
            dma((4, len(chunks))),
            dma((4, len(chunks))),
            dma((6, len(chunks))),
            dma((6, len(chunks))),
            dma((2 * ring - 1,)),
            dma((2 * ring - 1,)),
        ],
        compiler_params=pltpu.CompilerParams(
            collective_id=0, has_side_effects=True, vmem_limit_bytes=60 * 1024 * 1024
        ),
        name="window_attention",
    )(owners, owner_slot, counts, activations, stale_pairs, w_query, w_out)


def solution(mesh):
    placed = (
        P("seq", "head"),
        P("seq"),
        P("seq"),
        P("seq"),
        P(None, "seq", "head"),
        P(None, "head"),
        P("head", None),
    )
    return jax.shard_map(
        on_device, mesh=mesh, in_specs=placed, out_specs=P("seq", "head"), check_vma=False
    )
```

time: 76.5 us -> 75.1 us (0.982)
  the two profiles are of different devices: /device:TPU:1 before, /device:TPU:16 now
where the time goes in v4:
time: 75.1 us; the launch traced here: 74.9 us
  Pallas kernels  73.1 us (97%)
  local copies, waits for them, and re-layouts  1.78 us (2%)
    pallas_call x1, Pallas kernels, on_device(): pl.pallas_call(functools.partial(attention_kernel, seq_count, rows, chunk...  73.1 us
    unnamed x1, local copies, waits for them, and re-layouts  1.78 us

profile of v4, /device:TPU:16, one launch (start us, length us, event | category | flops | bytes accessed | tf_op | source)
XLA Modules:
  0.0 74.9 jit_solution(147835736639557796)
XLA Ops:
  0.0 73.1 %window_attention.1 = bf16[512,384]{1,0:T(8,128)(2,1)} custom-call(s32[2]{0:T(128)} %owners.1, s32[2]{0:T(128)} %owner_slot.1, s32[2]{0:T(128)} %counts.1, bf16[512,384]{1,0:T(8,128)(2,1)} %act_hbm.1, bf16[2,512,384]{2,1,0:T(8,128)(2,1)} %stale_hbm.1, bf16[1536,384]{1,0:T(8,128)(2,1)} %wq_hbm.1, bf16[384,1536]{1,0:T(8,128)(2,1)} %wo_hbm.1), custom_call_target="tpu_custom_call" | custom-call | tf_op jit(solution)/shard_map/window_attention/pallas_call | solution.py:481
  73.1 1.8 %copy.9 = bf16[512,384]{1,0:T(8,128)(2,1)} copy(bf16[512,384]{1,0:T(8,128)(2,1)} %window_attention.1) | data formatting | bytes 786432

commit v5 on v4

--- a/solution.py
+++ b/solution.py
@@ -115,10 +115,12 @@
     in_order = jnp.where(owner_slot[0] == 0, 1.0, 0.0).astype(F32)
     owner_1 = jnp.where(owner_slot[0] == 0, owners[1], owners[0])
     offset = lax.rem(owner_1 - seq + seq_count, seq_count)
+    odd = lax.rem(offset, 2)
+    offset = offset + odd * (1 - 2 * core)
     y_part = lax.rem(lax.div(offset, 2) + 4, ring)
     z_part = lax.rem(lax.div(offset + ring, plane) + 4, ring)
     digits = {
-        1: lax.rem(offset, 2),
+        1: odd,
         2: lax.rem(y_part, 3) - 1,
         6: lax.div(y_part, 3) - 1,
         plane: lax.rem(z_part, 3) - 1,
@@ -168,12 +170,13 @@
             src = moving.at[pl.ds(first_row(g, st), stream_rows)]
         else:
             src = landing.at[stage - 1, g, st, 0]
+        by = orders[st][stage]
         return remote(
             src,
             landing.at[stage, g, st, way],
             move_send.at[stage, g, st, way],
             move_recv.at[stage, g, st, way],
-            at_distance((1 - 2 * way) * orders[st][stage]),
+            other_core if by == 1 else at_distance((1 - 2 * way) * by),
         )
 
     def service(stage, g):
@@ -220,8 +223,6 @@
         for st in range(2):
             for way in range(ways(0)):
                 stride(0, g, st, way).start()
-    go_home.start()
-
     loads[1].wait()
     stage[...] = jnp.zeros_like(stage)
     row_ids = lax.broadcasted_iota(jnp.int32, (rows, width), 0)
@@ -255,9 +256,7 @@
 
     for g in range(groups):
         service(0, g)
-    go_home.wait_recv()
-    for way in range(2):
-        direct(0, way).start()
+    go_home.start()
 
     def lay_out(at, p, key, value):
         kcat[at, p] = jnp.transpose(key).astype(BF16)
@@ -382,6 +381,9 @@
         inner_copy(j, lax.rem(inner + ring - j, ring)).wait_recv()
     for j in range(1, ring):
         outer_copy(j, outer).start()
+    go_home.wait_recv()
+    for way in range(2):
+        direct(0, way).start()
     service(1, 0)
     service(1, 1)
     pass_on(0)

time: 75.1 us -> 75.6 us (level)
  the two profiles are of different devices: /device:TPU:16 before, /device:TPU:18 now
where the time goes in v5:
time: 75.6 us; the launch traced here: 75.4 us
  Pallas kernels  73.6 us (97%)
  local copies, waits for them, and re-layouts  1.78 us (2%)
    pallas_call x1, Pallas kernels, on_device(): pl.pallas_call(functools.partial(attention_kernel, seq_count, rows, chunk...  73.6 us
    unnamed x1, local copies, waits for them, and re-layouts  1.78 us

profile of v5, /device:TPU:18, one launch (start us, length us, event | category | flops | bytes accessed | tf_op | source)
XLA Modules:
  0.0 75.4 jit_solution(7230954575282095875)
XLA Ops:
  0.0 73.6 %window_attention.1 = bf16[512,384]{1,0:T(8,128)(2,1)} custom-call(s32[2]{0:T(128)} %owners.1, s32[2]{0:T(128)} %owner_slot.1, s32[2]{0:T(128)} %counts.1, bf16[512,384]{1,0:T(8,128)(2,1)} %act_hbm.1, bf16[2,512,384]{2,1,0:T(8,128)(2,1)} %stale_hbm.1, bf16[1536,384]{1,0:T(8,128)(2,1)} %wq_hbm.1, bf16[384,1536]{1,0:T(8,128)(2,1)} %wo_hbm.1), custom_call_target="tpu_custom_call" | custom-call | tf_op jit(solution)/shard_map/window_attention/pallas_call | solution.py:483
  73.6 1.8 %copy.9 = bf16[512,384]{1,0:T(8,128)(2,1)} copy(bf16[512,384]{1,0:T(8,128)(2,1)} %window_attention.1) | data formatting | bytes 786432

commit v6 on v5

--- a/solution.py
+++ b/solution.py
@@ -389,16 +389,14 @@
     pass_on(0)
     service(2, 0)
     service(2, 1)
+    service(3, 0)
+    service(3, 1)
     for j in range(1, ring):
         outer_copy(j, lax.rem(outer + ring - j, ring)).wait_recv()
     core_copy(core).start()
-    service(3, 0)
-    service(3, 1)
     for load in loads[2:]:
         load.wait()
     project_queries(0)
-    service(4, 0)
-    service(4, 1)
 
     core_copy(1 - core).wait_recv()
     for i in range(2):
@@ -418,17 +416,19 @@
         lay_out(2, p, pooled[0], pooled[1].astype(BF16))
 
     attend(0, 0, 0)
+    attend(0, 0, 1)
+    service(4, 0)
+    attend(0, 0, 2)
+    service(4, 1)
+    project_out(0)
     pass_on(1)
-    attend(0, 0, 1)
     pass_on(2)
-    attend(0, 0, 2)
-    project_out(0)
 
     project_queries(1)
+    relay(0)
     for p in range(pairs):
         attend(1, 1, p)
     project_out(1)
-    relay(0)
     project_queries(2)
     for p in range(pairs):
         attend(2, 1, p)

time: 75.6 us -> 77 us (1.019)
  the two profiles are of different devices: /device:TPU:18 before, /device:TPU:16 now
where the time goes in v6:
time: 77 us; the launch traced here: 76.8 us
  Pallas kernels  75 us (97%)
  local copies, waits for them, and re-layouts  1.78 us (2%)
    pallas_call x1, Pallas kernels, on_device(): pl.pallas_call(functools.partial(attention_kernel, seq_count, rows, chunk...  75 us
    unnamed x1, local copies, waits for them, and re-layouts  1.78 us

profile of v6, /device:TPU:16, one launch (start us, length us, event | category | flops | bytes accessed | tf_op | source)
XLA Modules:
  0.0 76.8 jit_solution(7237282786559365654)
XLA Ops:
  0.0 75.0 %window_attention.1 = bf16[512,384]{1,0:T(8,128)(2,1)} custom-call(s32[2]{0:T(128)} %owners.1, s32[2]{0:T(128)} %owner_slot.1, s32[2]{0:T(128)} %counts.1, bf16[512,384]{1,0:T(8,128)(2,1)} %act_hbm.1, bf16[2,512,384]{2,1,0:T(8,128)(2,1)} %stale_hbm.1, bf16[1536,384]{1,0:T(8,128)(2,1)} %wq_hbm.1, bf16[384,1536]{1,0:T(8,128)(2,1)} %wo_hbm.1), custom_call_target="tpu_custom_call" | custom-call | tf_op jit(solution)/shard_map/window_attention/pallas_call | solution.py:483
  75.0 1.8 %copy.9 = bf16[512,384]{1,0:T(8,128)(2,1)} copy(bf16[512,384]{1,0:T(8,128)(2,1)} %window_attention.1) | data formatting | bytes 786432

commit v7 on v4

--- a/solution.py
+++ b/solution.py
@@ -423,10 +423,10 @@
     project_out(0)
 
     project_queries(1)
+    relay(0)
     for p in range(pairs):
         attend(1, 1, p)
     project_out(1)
-    relay(0)
     project_queries(2)
     for p in range(pairs):
         attend(2, 1, p)

time: 75.1 us -> 75.3 us (level)
  the two profiles are of different devices: /device:TPU:16 before, /device:TPU:18 now
where the time goes in v7:
time: 75.3 us; the launch traced here: 75.2 us
  Pallas kernels  73.4 us (97%)
  local copies, waits for them, and re-layouts  1.78 us (2%)
    pallas_call x1, Pallas kernels, on_device(): pl.pallas_call(functools.partial(attention_kernel, seq_count, rows, chunk...  73.4 us
    unnamed x1, local copies, waits for them, and re-layouts  1.78 us

profile of v7, /device:TPU:18, one launch (start us, length us, event | category | flops | bytes accessed | tf_op | source)
XLA Modules:
  0.0 75.2 jit_solution(3832364957284570776)
XLA Ops:
  0.0 73.4 %window_attention.1 = bf16[512,384]{1,0:T(8,128)(2,1)} custom-call(s32[2]{0:T(128)} %owners.1, s32[2]{0:T(128)} %owner_slot.1, s32[2]{0:T(128)} %counts.1, bf16[512,384]{1,0:T(8,128)(2,1)} %act_hbm.1, bf16[2,512,384]{2,1,0:T(8,128)(2,1)} %stale_hbm.1, bf16[1536,384]{1,0:T(8,128)(2,1)} %wq_hbm.1, bf16[384,1536]{1,0:T(8,128)(2,1)} %wo_hbm.1), custom_call_target="tpu_custom_call" | custom-call | tf_op jit(solution)/shard_map/window_attention/pallas_call | solution.py:481
  73.4 1.8 %copy.9 = bf16[512,384]{1,0:T(8,128)(2,1)} copy(bf16[512,384]{1,0:T(8,128)(2,1)} %window_attention.1) | data formatting | bytes 786432
